TPU v7x, 512 devices: a whole 4x4x16 slice. The times are simulated.
512 devices in a mesh: section: 16 (over z_hi, y, core), seq: 32 (over z_lo, x).
Axes of the slice: x: 4, y: 4, z: 16 (z_hi: 2, z_lo: 8; z = z_hi * 8 + z_lo), core: 2. Of those that a mesh axis runs over, the one named last changes fastest.
Arguments:
- starting_carries: bfloat16 [32, 16, 128, 1024], P('seq', 'section'), may hold values from -9 to 9
- incoming_micro_loads: bfloat16 [2, 32, 2, 128, 1024], P(None, 'seq', None, None, 'section'), may hold values from -9 to 9
- layer_scaling_factor: float32 [16, 512], P('section'), may hold values from 0.1 to 1.9
- asking_matrix: bfloat16 [16, 512, 1024], P('section')
- lookup_matrix: bfloat16 [16, 512, 1024], P('section')
- content_matrix: bfloat16 [16, 512, 1024], P('section'), may hold values from -0.1875 to 0.1875
- emitting_matrix: bfloat16 [16, 512, 1024], P('section'), may hold values from -0.5 to 0.5
- rotation_turning: float32 [16, 5, 512], P('section'), may hold values from -1 to 1
- rotation_scaling: float32 [16, 5, 2, 512], P('section'), may hold values from 0.5 to 1.5
- higher_mate_lines: int32 [8, 5, 128], replicated, may hold values from 0 to 127, each once within a row
- piece_visibility_table: int32 [32, 2, 3], P('seq'), may hold values from 0 to 1, as said below
Outputs:
- emitted: bfloat16 [32, 16, 128, 1024], P('seq', 'section')
Inputs may be any that keep to these rules, and one draw needn't show every extreme that they name: `higher_mate_lines`: each row lists every number of 0 .. 127 once. `piece_visibility_table`: entry [j, 0, 2] is 1 for every j.
All inputs are finite; a program needn't handle non-finite values.
Results may differ from a plain program's by a relative error of at most 0.04.
Values may be sent and summed in bfloat16 or wider, within the bound.
A program may use at most 128 MiB of HBM per device.

v0:
```python
import jax
import jax.numpy as jnp
from jax import lax
from jax.sharding import PartitionSpec as P

HEADS = 16
WIN = 3
MIXES = 5
TICKS = 3


def from_partner(block, axis, bit):
    count = lax.axis_size(axis)
    route = []
    for low in range(count):
        high = low | 1 << bit
        if high != low and high < count:
            route += [(low, high), (high, low)]
    return lax.ppermute(block, axis, route)


def shifted(value, axis, by):
    devices = lax.axis_size(axis)
    pairs = [(i, i + by) for i in range(devices) if 0 <= i + by < devices]
    return lax.ppermute(value, axis, pairs)


def join_halves(mine, theirs, lower_here, axis_num):
    first = jnp.where(lower_here, mine, theirs)
    second = jnp.where(lower_here, theirs, mine)
    return jnp.concatenate([first, second], axis=axis_num)


def attention_layer(cascade_carry, gain, query_w, key_w, value_w, out_w, mask_row, half):
    block_num = 2 * lax.axis_index("seq") + half
    rows = cascade_carry.shape[0]
    head_size = query_w.shape[1] // HEADS
    wide = cascade_carry.astype(jnp.float32)
    square_mean = jnp.mean(wide * wide, axis=-1, keepdims=True)
    normed = (wide * lax.rsqrt(square_mean + 1e-06) * gain).astype(jnp.bfloat16)
    queries = jnp.dot(normed, query_w, preferred_element_type=jnp.float32).astype(jnp.bfloat16)
    keys_here = jnp.dot(normed, key_w, preferred_element_type=jnp.float32).astype(jnp.bfloat16)
    values_here = jnp.dot(normed, value_w, preferred_element_type=jnp.float32).astype(jnp.bfloat16)
    paired = jnp.stack([keys_here, values_here])
    sister = from_partner(paired, "section", 0)
    nearby = shifted(jnp.stack([paired, sister]), "seq", 1)
    near_own = nearby[0]
    near_sister = nearby[1]
    far_sister = shifted(sister, "seq", 2)
    upper_here = half == 1
    reach_one = jnp.where(upper_here, sister, near_sister)
    reach_three = jnp.where(upper_here, near_sister, far_sister)
    context = jnp.concatenate([reach_three, near_own, reach_one, paired], axis=1)
    context_keys = context[0].reshape((WIN + 1) * rows, HEADS, head_size)
    context_values = context[1].reshape((WIN + 1) * rows, HEADS, head_size)
    scores = (
        jnp.einsum(
            "qhd,khd->hqk",
            queries.reshape(rows, HEADS, head_size),
            context_keys,
            preferred_element_type=jnp.float32,
        )
        * 0.125
    )
    block_flags = []
    for place in range(WIN):
        reach = WIN - place
        block_flags.append(jnp.logical_and(block_num - reach >= 0, mask_row[reach - 1] == 1))
    earlier_ok = jnp.repeat(jnp.stack(block_flags), rows)
    earlier_ok = jnp.broadcast_to(earlier_ok[None, :], (rows, WIN * rows))
    rows_pos = jnp.arange(rows, dtype=jnp.int32)
    causal = rows_pos[None, :] <= rows_pos[:, None]
    allowed = jnp.concatenate([earlier_ok, causal], axis=1)
    scores = jnp.where(allowed[None], scores, jnp.float32(-1e30))
    top_score = jnp.max(scores, axis=-1, keepdims=True)
    expo = jnp.exp(scores - top_score)
    probs = (expo / jnp.sum(expo, axis=-1, keepdims=True)).astype(jnp.bfloat16)
    attended = jnp.einsum("hqk,khd->qhd", probs, context_values, preferred_element_type=jnp.float32)
    attended = attended.astype(jnp.bfloat16).reshape(rows, HEADS * head_size)
    return (wide + jnp.dot(attended, out_w, preferred_element_type=jnp.float32)).astype(
        jnp.bfloat16
    )


def pair_mix(wide, other, is_lower, angle_row, gain_pair):
    cosine = jnp.cos(angle_row)
    sine_part = jnp.sin(angle_row)
    new_lower = gain_pair[0] * (cosine * wide + sine_part * other)
    new_upper = gain_pair[1] * (cosine * wide - sine_part * other)
    return jnp.where(is_lower, new_lower, new_upper)


def butterfly_mix(cascade_carry, angles, gains, pairing, half):
    position = lax.axis_index("seq")
    count = lax.axis_size("seq")
    levels = (2 * count).bit_length() - 1
    lower_half = half == 0
    for layer in range(MIXES):
        bit_num = layer % levels
        if bit_num == 0:
            partner = from_partner(cascade_carry, "section", 0)
            is_lower = lower_half
        else:
            partner = from_partner(cascade_carry, "seq", bit_num - 1)
            is_lower = position // (1 << bit_num - 1) % 2 == 0
        ordering = pairing[layer]
        inverse = jnp.argsort(ordering)
        other = jnp.where(is_lower, partner[ordering], partner[inverse]).astype(jnp.float32)
        cascade_carry = pair_mix(
            cascade_carry.astype(jnp.float32), other, is_lower, angles[layer], gains[layer]
        ).astype(jnp.bfloat16)
    return cascade_carry


def local(
    starting_carries,
    incoming_micro_loads,
    layer_scaling_factor,
    asking_matrix,
    lookup_matrix,
    content_matrix,
    emitting_matrix,
    rotation_turning,
    rotation_scaling,
    higher_mate_lines,
    piece_visibility_table,
):
    slot = lax.axis_index("section")
    half = slot % 2
    section_num = slot // 2
    lower_here = half == 0
    theirs = (
        from_partner(asking_matrix[0], "section", 0),
        from_partner(lookup_matrix[0], "section", 0),
        from_partner(content_matrix[0], "section", 0),
        from_partner(emitting_matrix[0], "section", 0),
        from_partner(layer_scaling_factor[0].astype(jnp.bfloat16), "section", 0).astype(
            jnp.float32
        ),
        from_partner(rotation_turning[0].astype(jnp.bfloat16), "section", 0).astype(jnp.float32),
        from_partner(rotation_scaling[0].astype(jnp.bfloat16), "section", 0).astype(jnp.float32),
    )
    query_w = join_halves(asking_matrix[0], theirs[0], lower_here, 0)
    key_w = join_halves(lookup_matrix[0], theirs[1], lower_here, 0)
    value_w = join_halves(content_matrix[0], theirs[2], lower_here, 0)
    out_w = join_halves(emitting_matrix[0], theirs[3], lower_here, 0)
    gain = join_halves(layer_scaling_factor[0], theirs[4], lower_here, 0)
    angles = join_halves(rotation_turning[0], theirs[5], lower_here, 1)
    gains = join_halves(rotation_scaling[0], theirs[6], lower_here, 2)
    pairing = lax.dynamic_index_in_dim(higher_mate_lines, section_num, 0, keepdims=False)
    mask_row = lax.dynamic_index_in_dim(piece_visibility_table[0], half, 0, keepdims=False)
    fresh_all = lax.all_gather(incoming_micro_loads, "section", axis=4, tiled=True)
    fresh_here = lax.dynamic_index_in_dim(fresh_all[:, 0], half, 1, keepdims=False)
    first_section = section_num == 0
    cascade_carry = starting_carries[0, 0]
    for step_tick in range(TICKS):
        if step_tick > 0:
            moved = shifted(cascade_carry, "section", 2)
            cascade_carry = jnp.where(first_section, fresh_here[step_tick - 1], moved)
        cascade_carry = attention_layer(
            cascade_carry, gain, query_w, key_w, value_w, out_w, mask_row, half
        )
        cascade_carry = butterfly_mix(cascade_carry, angles, gains, pairing, half)
    return cascade_carry[None, None]


def solution(mesh):
    in_specs = (
        P("seq", "section", None, None),
        P(None, "seq", None, None, "section"),
        P("section", None),
        P("section", None, None),
        P("section", None, None),
        P("section", None, None),
        P("section", None, None),
        P("section", None, None),
        P("section", None, None, None),
        P(),
        P("seq", None, None),
    )
    out_specs = P("seq", "section", None, None)
    return jax.shard_map(local, mesh=mesh, in_specs=in_specs, out_specs=out_specs, check_vma=False)
```

profile of v0, /device:TPU:480, one launch (start us, length us, event | category | flops | bytes accessed | tf_op | source)
XLA Modules:
  0.0 518.6 jit_solution(11882030737539810243)
XLA Ops:
  9.9 2.4 collective-permute-start.1
  15.8 2.4 collective-permute-start.3
  25.4 2.5 sort.95
  27.9 2.5 sort.94
  32.9 2.5 sort.93
  35.5 2.4 collective-permute-start
  43.4 2.6 broadcast_select_fusion.3
  46.6 2.7 collective-permute-start.5
  51.9 3.4 collective-permute-start.6
  61.2 4.6 collective-permute-start.7
  65.8 2.8 broadcast_select_fusion.1
  68.6 32.2 %collective-permute-done.6 = bf16[2,2,128,1024]{3,2,1,0:T(8,128)(2,1)} collective-permute-done((bf16[2,2,128,1024]{3,2,1,0:T(8,128)(2,1)}, bf16[2,2,128,1024]{3,2,1,0:T(8,128)(2,1)}, u32[]{:S(2)}, u32[]{:S(2)}) %collective-permute-start.6) | collective-permute-done | bytes 1048608 | tf_op jit(solution)/shard_map/ppermute | solution.py:25
  104.7 3.5 fusion.104
  108.2 3.3 fusion.20
  117.7 12.2 %collective-permute-start.11 = (bf16[128,1024]{1,0:T(8,128)(2,1)S(1)}, bf16[128,1024]{1,0:T(8,128)(2,1)S(1)}, u32[]{:S(2)}, u32[]{:S(2)}) collective-permute-start(bf16[128,1024]{1,0:T(8,128)(2,1)S(1)} %select_convert_fusion.14), channel_id=1, source_target_pairs={{0,1},{1,0},{2,3},{3,2},{4,5},{5,4},{6,7},{7,6},{8,9},{9,8},{10,11... | collective-permute-start | bytes 786440 | tf_op jit(solution)/shard_map/ppermute | solution.py:19
  130.2 6.3 %collective-permute-done.11 = bf16[128,1024]{1,0:T(8,128)(2,1)S(1)} collective-permute-done((bf16[128,1024]{1,0:T(8,128)(2,1)S(1)}, bf16[128,1024]{1,0:T(8,128)(2,1)S(1)}, u32[]{:S(2)}, u32[]{:S(2)}) %collective-permute-start.11) | collective-permute-done | bytes 262176 | tf_op jit(solution)/shard_map/ppermute | solution.py:19
  138.5 2.4 collective-permute-start.12
  141.0 2.5 sort.96
  143.6 6.1 %collective-permute-done.12 = bf16[128,1024]{1,0:T(8,128)(2,1)S(1)} collective-permute-done((bf16[128,1024]{1,0:T(8,128)(2,1)S(1)}, bf16[128,1024]{1,0:T(8,128)(2,1)S(1)}, u32[]{:S(2)}, u32[]{:S(2)}) %collective-permute-start.12) | collective-permute-done | bytes 262176 | tf_op jit(solution)/shard_map/ppermute | solution.py:19
  153.7 2.5 sort.97
  156.4 4.1 collective-permute-done.13
  162.5 3.6 collective-permute-start.14
  166.3 10.6 %collective-permute-done.14 = bf16[128,1024]{1,0:T(8,128)(2,1)S(1)} collective-permute-done((bf16[128,1024]{1,0:T(8,128)(2,1)S(1)}, bf16[128,1024]{1,0:T(8,128)(2,1)S(1)}, u32[]{:S(2)}, u32[]{:S(2)}) %collective-permute-start.14) | collective-permute-done | bytes 262176 | tf_op jit(solution)/shard_map/ppermute | solution.py:19
  179.5 3.6 collective-permute-start.15
  183.2 2.3 constant_dynamic-slice_fusion.4
  185.9 15.1 %collective-permute-done.15 = bf16[128,1024]{1,0:T(8,128)(2,1)} collective-permute-done((bf16[128,1024]{1,0:T(8,128)(2,1)}, bf16[128,1024]{1,0:T(8,128)(2,1)}, u32[]{:S(2)}, u32[]{:S(2)}) %collective-permute-start.15) | collective-permute-done | bytes 262176 | tf_op jit(solution)/shard_map/ppermute | solution.py:25
  211.3 3.8 collective-permute-start.18
  217.4 46.1 %collective-permute-done.17 = bf16[2,2,128,1024]{3,2,1,0:T(8,128)(2,1)} collective-permute-done((bf16[2,2,128,1024]{3,2,1,0:T(8,128)(2,1)S(1)}, bf16[2,2,128,1024]{3,2,1,0:T(8,128)(2,1)}, u32[]{:S(2)}, u32[]{:S(2)}) %collective-permute-start.17) | collective-permute-done | bytes 1048608 | tf_op jit(solution)/shard_map/ppermute | solution.py:25
  268.1 4.7 fusion.105
  272.8 3.3 fusion.19
  282.2 12.6 %collective-permute-start.20 = (bf16[128,1024]{1,0:T(8,128)(2,1)S(1)}, bf16[128,1024]{1,0:T(8,128)(2,1)S(1)}, u32[]{:S(2)}, u32[]{:S(2)}) collective-permute-start(bf16[128,1024]{1,0:T(8,128)(2,1)S(1)} %select_convert_fusion.9), channel_id=1, source_target_pairs={{0,1},{1,0},{2,3},{3,2},{4,5},{5,4},{6,7},{7,6},{8,9},{9,8},{10,11... | collective-permute-start | bytes 786440 | tf_op jit(solution)/shard_map/ppermute | solution.py:19
  294.8 6.4 %collective-permute-done.20 = bf16[128,1024]{1,0:T(8,128)(2,1)S(1)} collective-permute-done((bf16[128,1024]{1,0:T(8,128)(2,1)S(1)}, bf16[128,1024]{1,0:T(8,128)(2,1)S(1)}, u32[]{:S(2)}, u32[]{:S(2)}) %collective-permute-start.20) | collective-permute-done | bytes 262176 | tf_op jit(solution)/shard_map/ppermute | solution.py:19
  305.3 9.3 %collective-permute-done.21 = bf16[128,1024]{1,0:T(8,128)(2,1)S(1)} collective-permute-done((bf16[128,1024]{1,0:T(8,128)(2,1)S(1)}, bf16[128,1024]{1,0:T(8,128)(2,1)S(1)}, u32[]{:S(2)}, u32[]{:S(2)}) %collective-permute-start.21) | collective-permute-done | bytes 262176 | tf_op jit(solution)/shard_map/ppermute | solution.py:19
  316.8 5.1 collective-permute-start.22
  321.9 5.2 collective-permute-done.22
  331.2 12.8 %collective-permute-done.23 = bf16[128,1024]{1,0:T(8,128)(2,1)S(1)} collective-permute-done((bf16[128,1024]{1,0:T(8,128)(2,1)S(1)}, bf16[128,1024]{1,0:T(8,128)(2,1)S(1)}, u32[]{:S(2)}, u32[]{:S(2)}) %collective-permute-start.23) | collective-permute-done | bytes 262176 | tf_op jit(solution)/shard_map/ppermute | solution.py:19
  350.3 18.2 %collective-permute-done.24 = bf16[128,1024]{1,0:T(8,128)(2,1)S(1)} collective-permute-done((bf16[128,1024]{1,0:T(8,128)(2,1)}, bf16[128,1024]{1,0:T(8,128)(2,1)S(1)}, u32[]{:S(2)}, u32[]{:S(2)}) %collective-permute-start.24) | collective-permute-done | bytes 262176 | tf_op jit(solution)/shard_map/ppermute | solution.py:25
  375.4 2.6 collective-permute-start.26
  378.0 3.4 collective-permute-start.27
  384.5 44.4 %collective-permute-done.26 = bf16[2,2,128,1024]{3,2,1,0:T(8,128)(2,1)S(1)} collective-permute-done((bf16[2,2,128,1024]{3,2,1,0:T(8,128)(2,1)S(1)}, bf16[2,2,128,1024]{3,2,1,0:T(8,128)(2,1)S(1)}, u32[]{:S(2)}, u32[]{:S(2)}) %collective-permute-start.26) | collective-permute-done | bytes 1048608 | tf_op jit(solution)/shard_map/ppermute | solution.py:25
  431.6 4.5 fusion.106
  436.1 3.3 fusion.18
  445.5 13.7 %collective-permute-start.29 = (bf16[128,1024]{1,0:T(8,128)(2,1)S(1)}, bf16[128,1024]{1,0:T(8,128)(2,1)S(1)}, u32[]{:S(2)}, u32[]{:S(2)}) collective-permute-start(bf16[128,1024]{1,0:T(8,128)(2,1)S(1)} %select_convert_fusion.4), channel_id=1, source_target_pairs={{0,1},{1,0},{2,3},{3,2},{4,5},{5,4},{6,7},{7,6},{8,9},{9,8},{10,11... | collective-permute-start | bytes 786440 | tf_op jit(solution)/shard_map/ppermute | solution.py:19
  459.2 6.6 %collective-permute-done.29 = bf16[128,1024]{1,0:T(8,128)(2,1)S(1)} collective-permute-done((bf16[128,1024]{1,0:T(8,128)(2,1)S(1)}, bf16[128,1024]{1,0:T(8,128)(2,1)S(1)}, u32[]{:S(2)}, u32[]{:S(2)}) %collective-permute-start.29) | collective-permute-done | bytes 262176 | tf_op jit(solution)/shard_map/ppermute | solution.py:19
  470.1 9.1 %collective-permute-done.30 = bf16[128,1024]{1,0:T(8,128)(2,1)S(1)} collective-permute-done((bf16[128,1024]{1,0:T(8,128)(2,1)S(1)}, bf16[128,1024]{1,0:T(8,128)(2,1)S(1)}, u32[]{:S(2)}, u32[]{:S(2)}) %collective-permute-start.30) | collective-permute-done | bytes 262176 | tf_op jit(solution)/shard_map/ppermute | solution.py:19
  481.4 5.1 collective-permute-start.31
  486.5 5.2 collective-permute-done.31
  495.9 12.8 %collective-permute-done.32 = bf16[128,1024]{1,0:T(8,128)(2,1)S(1)} collective-permute-done((bf16[128,1024]{1,0:T(8,128)(2,1)S(1)}, bf16[128,1024]{1,0:T(8,128)(2,1)S(1)}, u32[]{:S(2)}, u32[]{:S(2)}) %collective-permute-start.32) | collective-permute-done | bytes 262176 | tf_op jit(solution)/shard_map/ppermute | solution.py:19
  (283 shorter events, 121.9 us)
Async XLA Ops:
  6.5 35.5 %copy-start.27 = (bf16[1,1,128,1024]{3,2,1,0:T(8,128)(2,1)S(1)}, bf16[1,1,128,1024]{3,2,1,0:T(8,128)(2,1)}, u32[]{:S(2)}) copy-start(bf16[1,1,128,1024]{3,2,1,0:T(8,128)(2,1)} %param.11) | copy-start | bytes 786436
  6.5 176.7 %all-gather.2.cloned.1.call-start = ((), (), s32[]{:S(2)}) async-start(), calls=%async_computation | async-start | bytes 1114112 | tf_op jit(solution)/shard_map/all_gather | solution.py:152
  7.3 28.2 %collective-permute-start.2 = (bf16[512]{0:T(512)(128)(2,1)S(1)}, bf16[512]{0:T(512)(128)(2,1)S(1)}, u32[]{:S(2)}, u32[]{:S(2)}) collective-permute-start(bf16[512]{0:T(512)(128)(2,1)S(1)} %convert_element_type.243), channel_id=1, source_target_pairs={{0,32},{32,0},{64,96},{96,64},{128,160},{160,128},{192,224},{224,1... | collective-permute-start | bytes 3080 | tf_op jit(solution)/shard_map/ppermute | solution.py:19
  9.9 47.4 %collective-permute-start.1 = (bf16[5,512]{1,0:T(8,128)(2,1)S(1)}, bf16[5,512]{1,0:T(8,128)(2,1)S(1)}, u32[]{:S(2)}, u32[]{:S(2)}) collective-permute-start(bf16[5,512]{1,0:T(8,128)(2,1)S(1)} %bitcast.253), channel_id=1, source_target_pairs={{0,32},{32,0},{64,96},{96,64},{128,160},{160,128},{192,224},{224,1... | collective-permute-start | bytes 15368 | tf_op jit(solution)/shard_map/ppermute | solution.py:19
  13.9 28.7 %collective-permute-start.4 = (bf16[512,1024]{1,0:T(8,128)(2,1)}, bf16[512,1024]{1,0:T(8,128)(2,1)S(1)}, u32[]{:S(2)}, u32[]{:S(2)}) collective-permute-start(bf16[512,1024]{1,0:T(8,128)(2,1)} %bitcast.182), channel_id=1, source_target_pairs={{0,32},{32,0},{64,96},{96,64},{128,160},{160,128},{192,224},{224,1... | collective-permute-start | bytes 3145736 | tf_op jit(solution)/shard_map/ppermute | solution.py:19
  15.8 22.8 %collective-permute-start.3 = (bf16[512,1024]{1,0:T(8,128)(2,1)}, bf16[512,1024]{1,0:T(8,128)(2,1)S(1)}, u32[]{:S(2)}, u32[]{:S(2)}) collective-permute-start(bf16[512,1024]{1,0:T(8,128)(2,1)} %bitcast.180), channel_id=1, source_target_pairs={{0,32},{32,0},{64,96},{96,64},{128,160},{160,128},{192,224},{224,1... | collective-permute-start | bytes 3145736 | tf_op jit(solution)/shard_map/ppermute | solution.py:19
  18.2 25.2 %collective-permute-start.8 = (bf16[512,1024]{1,0:T(8,128)(2,1)}, bf16[512,1024]{1,0:T(8,128)(2,1)}, u32[]{:S(2)}, u32[]{:S(2)}) collective-permute-start(bf16[512,1024]{1,0:T(8,128)(2,1)} %bitcast.181), channel_id=1, source_target_pairs={{0,32},{32,0},{64,96},{96,64},{128,160},{160,128},{192,224},{224,1... | collective-permute-start | bytes 3145736 | tf_op jit(solution)/shard_map/ppermute | solution.py:19
  21.3 24.7 %copy-start.54 = (f32[128]{0:T(128)}, f32[128]{0:T(128)S(1)}, u32[]{:S(2)}) copy-start(f32[128]{0:T(128)S(1)} %add_rsqrt_fusion.2) | copy-start | bytes 1540
  35.5 78.5 %collective-permute-start = (bf16[5,2,512]{2,1,0:T(2,128)(2,1)}, bf16[5,2,512]{2,1,0:T(2,128)(2,1)}, u32[]{:S(2)}, u32[]{:S(2)}) collective-permute-start(bf16[5,2,512]{2,1,0:T(2,128)(2,1)} %bitcast_convert_fusion), channel_id=1, source_target_pairs={{0,32},{32,0},{64,96},{96,64},{128,160},{160,128},{192,224},{224,1... | collective-permute-start | bytes 30728 | tf_op jit(solution)/shard_map/ppermute | solution.py:19
  38.6 27.2 %collective-permute-start.9 = (bf16[512,1024]{1,0:T(8,128)(2,1)}, bf16[512,1024]{1,0:T(8,128)(2,1)}, u32[]{:S(2)}, u32[]{:S(2)}) collective-permute-start(bf16[512,1024]{1,0:T(8,128)(2,1)} %bitcast.183), channel_id=1, source_target_pairs={{0,32},{32,0},{64,96},{96,64},{128,160},{160,128},{192,224},{224,1... | collective-permute-start | bytes 3145736 | tf_op jit(solution)/shard_map/ppermute | solution.py:19
  46.5 19.3 %copy-start.4 = (bf16[1,512,1024]{2,1,0:T(8,128)(2,1)S(1)}, bf16[1,512,1024]{2,1,0:T(8,128)(2,1)}, u32[]{:S(2)}) copy-start(bf16[1,512,1024]{2,1,0:T(8,128)(2,1)} %param.17) | copy-start | bytes 3145732
  46.6 4.2 collective-permute-start.5
  51.9 48.9 %collective-permute-start.6 = (bf16[2,2,128,1024]{3,2,1,0:T(8,128)(2,1)}, bf16[2,2,128,1024]{3,2,1,0:T(8,128)(2,1)}, u32[]{:S(2)}, u32[]{:S(2)}) collective-permute-start(bf16[2,2,128,1024]{3,2,1,0:T(8,128)(2,1)} %pad_maximum_fusion.4), channel_id=1, source_target_pairs={{0,1},{1,2},{2,3},{3,4},{4,5},{5,6},{6,7},{7,8},{8,9},{9,10},{10,1... | collective-permute-start | bytes 3145736 | tf_op jit(solution)/shard_map/ppermute | solution.py:25
  60.3 42.7 %copy-start.25 = (bf16[1,128,1024]{2,1,0:T(8,128)(2,1)S(1)}, bf16[1,128,1024]{2,1,0:T(8,128)(2,1)}, u32[]{:S(2)}) copy-start(bf16[1,128,1024]{2,1,0:T(8,128)(2,1)} %copy-done.24) | copy-start | bytes 786436
  61.2 40.7 %collective-permute-start.7 = (bf16[2,128,1024]{2,1,0:T(8,128)(2,1)S(1)}, bf16[2,128,1024]{2,1,0:T(8,128)(2,1)S(1)}, u32[]{:S(2)}, u32[]{:S(2)}) collective-permute-start(bf16[2,128,1024]{2,1,0:T(8,128)(2,1)S(1)} %collective-permute-done.5), channel_id=1, source_target_pairs={{0,2},{1,3},{2,4},{3,5},{4,6},{5,7},{6,8},{7,9},{8,10},{9,11},{10,... | collective-permute-start | bytes 1572872 | tf_op jit(solution)/shard_map/ppermute | solution.py:25
  112.1 3.4 collective-permute-start.10
  116.5 24.4 %copy-start.48 = (s32[128]{0:T(128)S(1)}, s32[128]{0:T(128)}, u32[]{:S(2)}) copy-start(s32[128]{0:T(128)} %get-tuple-element.83) | copy-start | bytes 1540
  116.5 24.5 %copy-start.53 = (s32[128]{0:T(128)S(1)}, s32[128]{0:T(128)}, u32[]{:S(2)}) copy-start(s32[128]{0:T(128)} %get-tuple-element.77) | copy-start | bytes 1540
  117.7 18.8 %collective-permute-start.11 = (bf16[128,1024]{1,0:T(8,128)(2,1)S(1)}, bf16[128,1024]{1,0:T(8,128)(2,1)S(1)}, u32[]{:S(2)}, u32[]{:S(2)}) collective-permute-start(bf16[128,1024]{1,0:T(8,128)(2,1)S(1)} %select_convert_fusion.14), channel_id=1, source_target_pairs={{0,1},{1,0},{2,3},{3,2},{4,5},{5,4},{6,7},{7,6},{8,9},{9,8},{10,11... | collective-permute-start | bytes 786440 | tf_op jit(solution)/shard_map/ppermute | solution.py:19
  130.0 21.5 %copy-start.35 = (s32[1024]{0:T(1024)}, s32[1024]{0:T(1024)S(1)}, u32[]{:S(2)}) copy-start(s32[1024]{0:T(1024)S(1)} %pad_clamp_fusion.6) | copy-start | bytes 12292
  130.0 19.7 %copy-start.36 = (s32[1024]{0:T(1024)}, s32[1024]{0:T(1024)S(1)}, u32[]{:S(2)}) copy-start(s32[1024]{0:T(1024)S(1)} %pad_clamp_fusion.4) | copy-start | bytes 12292
  138.5 11.2 %collective-permute-start.12 = (bf16[128,1024]{1,0:T(8,128)(2,1)S(1)}, bf16[128,1024]{1,0:T(8,128)(2,1)S(1)}, u32[]{:S(2)}, u32[]{:S(2)}) collective-permute-start(bf16[128,1024]{1,0:T(8,128)(2,1)S(1)} %select_convert_fusion.13), channel_id=1, source_target_pairs={{0,2},{2,0},{1,3},{3,1},{4,6},{6,4},{5,7},{7,5},{8,10},{10,8},{9,1... | collective-permute-start | bytes 786440 | tf_op jit(solution)/shard_map/ppermute | solution.py:19
  151.7 8.8 %collective-permute-start.13 = (bf16[128,1024]{1,0:T(8,128)(2,1)S(1)}, bf16[128,1024]{1,0:T(8,128)(2,1)S(1)}, u32[]{:S(2)}, u32[]{:S(2)}) collective-permute-start(bf16[128,1024]{1,0:T(8,128)(2,1)S(1)} %select_convert_fusion.12), channel_id=1, source_target_pairs={{0,4},{4,0},{1,5},{5,1},{2,6},{6,2},{3,7},{7,3},{8,12},{12,8},{9,1... | collective-permute-start | bytes 786440 | tf_op jit(solution)/shard_map/ppermute | solution.py:19
  162.5 14.4 %collective-permute-start.14 = (bf16[128,1024]{1,0:T(8,128)(2,1)S(1)}, bf16[128,1024]{1,0:T(8,128)(2,1)S(1)}, u32[]{:S(2)}, u32[]{:S(2)}) collective-permute-start(bf16[128,1024]{1,0:T(8,128)(2,1)S(1)} %select_convert_fusion.11), channel_id=1, source_target_pairs={{0,8},{8,0},{1,9},{9,1},{2,10},{10,2},{3,11},{11,3},{4,12},{12,4},... | collective-permute-start | bytes 786440 | tf_op jit(solution)/shard_map/ppermute | solution.py:19
  179.5 24.8 %copy-start.11 = (bf16[512,1024]{1,0:T(8,128)(2,1)S(1)}, bf16[512,1024]{1,0:T(8,128)(2,1)}, u32[]{:S(2)}) copy-start(bf16[512,1024]{1,0:T(8,128)(2,1)} %copy-done.10) | copy-start | bytes 3145732
  179.5 24.8 %copy-start.14 = (bf16[512,1024]{1,0:T(8,128)(2,1)S(1)}, bf16[512,1024]{1,0:T(8,128)(2,1)}, u32[]{:S(2)}) copy-start(bf16[512,1024]{1,0:T(8,128)(2,1)} %copy-done.13) | copy-start | bytes 3145732
  179.5 21.5 %collective-permute-start.15 = (bf16[128,1024]{1,0:T(8,128)(2,1)}, bf16[128,1024]{1,0:T(8,128)(2,1)}, u32[]{:S(2)}, u32[]{:S(2)}) collective-permute-start(bf16[128,1024]{1,0:T(8,128)(2,1)} %select_convert_fusion.10), channel_id=1, source_target_pairs={{0,64},{32,96},{64,128},{96,160},{128,192},{160,224},{192,256},{22... | collective-permute-start | bytes 786440 | tf_op jit(solution)/shard_map/ppermute | solution.py:25
  204.9 3.9 collective-permute-start.16
  209.0 54.5 %collective-permute-start.17 = (bf16[2,2,128,1024]{3,2,1,0:T(8,128)(2,1)S(1)}, bf16[2,2,128,1024]{3,2,1,0:T(8,128)(2,1)}, u32[]{:S(2)}, u32[]{:S(2)}) collective-permute-start(bf16[2,2,128,1024]{3,2,1,0:T(8,128)(2,1)S(1)} %pad_maximum_fusion.5), channel_id=1, source_target_pairs={{0,1},{1,2},{2,3},{3,4},{4,5},{5,6},{6,7},{7,8},{8,9},{9,10},{10,1... | collective-permute-start | bytes 3145736 | tf_op jit(solution)/shard_map/ppermute | solution.py:25
  211.3 53.3 %collective-permute-start.18 = (bf16[2,128,1024]{2,1,0:T(8,128)(2,1)S(1)}, bf16[2,128,1024]{2,1,0:T(8,128)(2,1)S(1)}, u32[]{:S(2)}, u32[]{:S(2)}) collective-permute-start(bf16[2,128,1024]{2,1,0:T(8,128)(2,1)S(1)} %collective-permute-done.16), channel_id=1, source_target_pairs={{0,2},{1,3},{2,4},{3,5},{4,6},{5,7},{6,8},{7,9},{8,10},{9,11},{10,... | collective-permute-start | bytes 1572872 | tf_op jit(solution)/shard_map/ppermute | solution.py:25
  276.6 3.4 collective-permute-start.19
  282.2 19.0 %collective-permute-start.20 = (bf16[128,1024]{1,0:T(8,128)(2,1)S(1)}, bf16[128,1024]{1,0:T(8,128)(2,1)S(1)}, u32[]{:S(2)}, u32[]{:S(2)}) collective-permute-start(bf16[128,1024]{1,0:T(8,128)(2,1)S(1)} %select_convert_fusion.9), channel_id=1, source_target_pairs={{0,1},{1,0},{2,3},{3,2},{4,5},{5,4},{6,7},{7,6},{8,9},{9,8},{10,11... | collective-permute-start | bytes 786440 | tf_op jit(solution)/shard_map/ppermute | solution.py:19
  303.4 11.2 %collective-permute-start.21 = (bf16[128,1024]{1,0:T(8,128)(2,1)S(1)}, bf16[128,1024]{1,0:T(8,128)(2,1)S(1)}, u32[]{:S(2)}, u32[]{:S(2)}) collective-permute-start(bf16[128,1024]{1,0:T(8,128)(2,1)S(1)} %select_convert_fusion.8), channel_id=1, source_target_pairs={{0,2},{2,0},{1,3},{3,1},{4,6},{6,4},{5,7},{7,5},{8,10},{10,8},{9,1... | collective-permute-start | bytes 786440 | tf_op jit(solution)/shard_map/ppermute | solution.py:19
  316.8 10.3 %collective-permute-start.22 = (bf16[128,1024]{1,0:T(8,128)(2,1)S(1)}, bf16[128,1024]{1,0:T(8,128)(2,1)S(1)}, u32[]{:S(2)}, u32[]{:S(2)}) collective-permute-start(bf16[128,1024]{1,0:T(8,128)(2,1)S(1)} %select_convert_fusion.7), channel_id=1, source_target_pairs={{0,4},{4,0},{1,5},{5,1},{2,6},{6,2},{3,7},{7,3},{8,12},{12,8},{9,1... | collective-permute-start | bytes 786440 | tf_op jit(solution)/shard_map/ppermute | solution.py:19
  329.3 14.7 %collective-permute-start.23 = (bf16[128,1024]{1,0:T(8,128)(2,1)S(1)}, bf16[128,1024]{1,0:T(8,128)(2,1)S(1)}, u32[]{:S(2)}, u32[]{:S(2)}) collective-permute-start(bf16[128,1024]{1,0:T(8,128)(2,1)S(1)} %select_convert_fusion.6), channel_id=1, source_target_pairs={{0,8},{8,0},{1,9},{9,1},{2,10},{10,2},{3,11},{11,3},{4,12},{12,4},... | collective-permute-start | bytes 786440 | tf_op jit(solution)/shard_map/ppermute | solution.py:19
  345.0 25.7 %copy-start.12 = (bf16[512,1024]{1,0:T(8,128)(2,1)S(1)}, bf16[512,1024]{1,0:T(8,128)(2,1)}, u32[]{:S(2)}) copy-start(bf16[512,1024]{1,0:T(8,128)(2,1)} %copy-done.10) | copy-start | bytes 3145732
  345.0 25.7 %copy-start.15 = (bf16[512,1024]{1,0:T(8,128)(2,1)S(1)}, bf16[512,1024]{1,0:T(8,128)(2,1)}, u32[]{:S(2)}) copy-start(bf16[512,1024]{1,0:T(8,128)(2,1)} %copy-done.13) | copy-start | bytes 3145732
  348.0 20.5 %collective-permute-start.24 = (bf16[128,1024]{1,0:T(8,128)(2,1)}, bf16[128,1024]{1,0:T(8,128)(2,1)S(1)}, u32[]{:S(2)}, u32[]{:S(2)}) collective-permute-start(bf16[128,1024]{1,0:T(8,128)(2,1)} %select_convert_fusion.5), channel_id=1, source_target_pairs={{0,64},{32,96},{64,128},{96,160},{128,192},{160,224},{192,256},{22... | collective-permute-start | bytes 786440 | tf_op jit(solution)/shard_map/ppermute | solution.py:25
  350.3 20.5 %copy-start.45 = (f32[1024]{0:T(1024)S(1)}, f32[1024]{0:T(1024)}, u32[]{:S(2)}) copy-start(f32[1024]{0:T(1024)} %copy-done.43) | copy-start | bytes 12292
  371.4 3.9 collective-permute-start.25
  375.4 53.4 %collective-permute-start.26 = (bf16[2,2,128,1024]{3,2,1,0:T(8,128)(2,1)S(1)}, bf16[2,2,128,1024]{3,2,1,0:T(8,128)(2,1)S(1)}, u32[]{:S(2)}, u32[]{:S(2)}) collective-permute-start(bf16[2,2,128,1024]{3,2,1,0:T(8,128)(2,1)S(1)} %pad_maximum_fusion.6), channel_id=1, source_target_pairs={{0,1},{1,2},{2,3},{3,4},{4,5},{5,6},{6,7},{7,8},{8,9},{9,10},{10,1... | collective-permute-start | bytes 3145736 | tf_op jit(solution)/shard_map/ppermute | solution.py:25
  378.0 50.8 %collective-permute-start.27 = (bf16[2,128,1024]{2,1,0:T(8,128)(2,1)S(1)}, bf16[2,128,1024]{2,1,0:T(8,128)(2,1)}, u32[]{:S(2)}, u32[]{:S(2)}) collective-permute-start(bf16[2,128,1024]{2,1,0:T(8,128)(2,1)S(1)} %collective-permute-done.25), channel_id=1, source_target_pairs={{0,2},{1,3},{2,4},{3,5},{4,6},{5,7},{6,8},{7,9},{8,10},{9,11},{10,... | collective-permute-start | bytes 1572872 | tf_op jit(solution)/shard_map/ppermute | solution.py:25
  439.9 3.4 collective-permute-start.28
  445.5 20.3 %collective-permute-start.29 = (bf16[128,1024]{1,0:T(8,128)(2,1)S(1)}, bf16[128,1024]{1,0:T(8,128)(2,1)S(1)}, u32[]{:S(2)}, u32[]{:S(2)}) collective-permute-start(bf16[128,1024]{1,0:T(8,128)(2,1)S(1)} %select_convert_fusion.4), channel_id=1, source_target_pairs={{0,1},{1,0},{2,3},{3,2},{4,5},{5,4},{6,7},{7,6},{8,9},{9,8},{10,11... | collective-permute-start | bytes 786440 | tf_op jit(solution)/shard_map/ppermute | solution.py:19
  468.0 11.2 %collective-permute-start.30 = (bf16[128,1024]{1,0:T(8,128)(2,1)S(1)}, bf16[128,1024]{1,0:T(8,128)(2,1)S(1)}, u32[]{:S(2)}, u32[]{:S(2)}) collective-permute-start(bf16[128,1024]{1,0:T(8,128)(2,1)S(1)} %select_convert_fusion.3), channel_id=1, source_target_pairs={{0,2},{2,0},{1,3},{3,1},{4,6},{6,4},{5,7},{7,5},{8,10},{10,8},{9,1... | collective-permute-start | bytes 786440 | tf_op jit(solution)/shard_map/ppermute | solution.py:19
  481.4 10.3 %collective-permute-start.31 = (bf16[128,1024]{1,0:T(8,128)(2,1)S(1)}, bf16[128,1024]{1,0:T(8,128)(2,1)S(1)}, u32[]{:S(2)}, u32[]{:S(2)}) collective-permute-start(bf16[128,1024]{1,0:T(8,128)(2,1)S(1)} %select_convert_fusion.2), channel_id=1, source_target_pairs={{0,4},{4,0},{1,5},{5,1},{2,6},{6,2},{3,7},{7,3},{8,12},{12,8},{9,1... | collective-permute-start | bytes 786440 | tf_op jit(solution)/shard_map/ppermute | solution.py:19
  491.7 19.9 %copy-start.1 = (s32[1,2,3]{2,1,0:T(2,128)S(1)}, s32[1,2,3]{2,1,0:T(2,128)}, u32[]{:S(2)}) copy-start(s32[1,2,3]{2,1,0:T(2,128)} %param.21) | copy-start | bytes 76
  494.0 14.7 %collective-permute-start.32 = (bf16[128,1024]{1,0:T(8,128)(2,1)S(1)}, bf16[128,1024]{1,0:T(8,128)(2,1)S(1)}, u32[]{:S(2)}, u32[]{:S(2)}) collective-permute-start(bf16[128,1024]{1,0:T(8,128)(2,1)S(1)} %select_convert_fusion.1), channel_id=1, source_target_pairs={{0,8},{8,0},{1,9},{9,1},{2,10},{10,2},{3,11},{11,3},{4,12},{12,4},... | collective-permute-start | bytes 786440 | tf_op jit(solution)/shard_map/ppermute | solution.py:19
  (41 other events, 384.2 us)
Sparse Core Ops, SparseCore 0:
  14.0 74.0 all-gather.1
where the time goes:
time: 529 us; the launch traced here: 519 us
  waiting for transfers between devices  259 us (49%)
  starting transfers between devices  118 us (22%)
  local copies, waits for them, and re-layouts  48.2 us (9%)
  other arithmetic  42.2 us (8%)
  matrix products  34.5 us (7%)
  between operations  17.2 us (3%)
    ppermute x8, waiting for transfers between devices, shifted(): return lax.ppermute(value, axis, pairs)  156 us
    ppermute x25, waiting for transfers between devices, from_partner(): return lax.ppermute(block, axis, route)  103 us
    ppermute x25, starting transfers between devices, from_partner(): return lax.ppermute(block, axis, route)  92 us
    ppermute x8, starting transfers between devices, shifted(): return lax.ppermute(value, axis, pairs)  25.6 us
    gather x15, local copies, waits for them, and re-layouts, butterfly_mix(): partner[ordering]  14.4 us
    gather x15, local copies, waits for them, and re-layouts, butterfly_mix(): partner[inverse]  14.4 us
    sub x3, matrix products, attention_layer(): expo = jnp.exp(scores - top_score)  12.7 us
    sort x5, other arithmetic, butterfly_mix(): inverse = jnp.argsort(ordering)  12.7 us
  transfers between devices with their start and end apart: 34, of which 23 were waited for; matrix products, arithmetic and copies ran while one was open for 13% of the time, Pallas kernels for 0%

commit v1 on v0

v1 whole, which is shorter than its diff:
```python
import jax
import jax.numpy as jnp
from jax import lax
from jax.experimental import pallas as pl
from jax.experimental.pallas import tpu as pltpu
from jax.sharding import PartitionSpec as P

HEADS = 16
WIN = 3
MIXES = 5
TICKS = 3
ROWS = 128
CHUNK = 128
CHUNKS = 8
WIDE = 1024
HALO_PARTS = 2
PER_PART = CHUNKS // HALO_PARTS
BF = jnp.bfloat16
F32 = jnp.float32


def remote(src, dst, send_sem, recv_sem, section, seq):
    return pltpu.make_async_remote_copy(
        src_ref=src,
        dst_ref=dst,
        send_sem=send_sem,
        recv_sem=recv_sem,
        device_id={"section": section, "seq": seq},
        device_id_type=pl.DeviceIdType.MESH,
    )


def kernel(
    start_ref, fresh_ref, gain_ref, wq_ref, wk_ref, wv_ref, wo_ref, angle_ref, scale_ref,
    pairing_ref, table_ref,
    out_ref,
    weights, gains, angles, scales, entering, halo, normed, queries, keys, values, attended,
    mixed, row_in, row_out, col_in, col_out, onehot, coef, bias, fresh_in, fresh_full,
    weight_local, weight_send, weight_recv, param_local, param_send, param_recv,
    fresh_send, fresh_recv, full_send,
    halo_send, halo_recv, row_send, row_recv, col_send, col_recv, back_send, back_recv,
):
    slot = lax.axis_index("section")
    seq = lax.axis_index("seq")
    section = slot // 2
    half = slot % 2
    sister = slot + 1 - 2 * half
    x = seq % 4
    z = seq // 4
    zrow = z % 4
    zbase = z - zrow
    mine = 2 * x + half
    held = (zrow + x) % 4

    weight_refs = (wk_ref, wv_ref, wq_ref, wo_ref)
    place = pl.ds(pl.multiple_of(half * 512, 512), 512)
    local_weights = [
        pltpu.make_async_copy(ref.at[0], weights.at[k, place], weight_local.at[k])
        for k, ref in enumerate(weight_refs)
    ]
    param_pairs = (
        (gain_ref, gains.at[half]),
        (angle_ref.at[0], angles.at[half]),
        (scale_ref.at[0], scales.at[half]),
    )
    local_params = [
        pltpu.make_async_copy(src, dst, param_local.at[k]) for k, (src, dst) in enumerate(param_pairs)
    ]
    for copy in local_weights + local_params:
        copy.start()

    @pl.when(seq < 2)
    def _():
        halo[...] = jnp.zeros_like(halo)

    barrier = pltpu.get_barrier_semaphore()

    def greet(to_section, to_seq):
        pl.semaphore_signal(
            barrier, inc=1, device_id={"section": to_section, "seq": to_seq},
            device_id_type=pl.DeviceIdType.MESH,
        )

    for k in range(1, CHUNKS):
        peer = (mine + k) % CHUNKS
        greet(2 * section + peer % 2, 4 * z + peer // 2)
    for k in range(1, 4):
        greet(slot, 4 * (zbase + (zrow + k) % 4) + x)
    for k in range(CHUNKS):
        source = (mine + k) % CHUNKS
        source_seq = 4 * (zbase + (x - source // 2 + 4) % 4) + source // 2

        @pl.when(section > 0)
        def _():
            greet(2 * section - 2 + source % 2, source_seq)

        if k == 0:
            @pl.when(zrow > 0)
            def _():
                greet(2 * section + source % 2, source_seq)
        else:
            greet(2 * section + source % 2, source_seq)

    @pl.when(seq > 0)
    def _():
        greet(slot, seq - 1)

    has_extra = jnp.logical_or(half == 1, seq >= 2)
    gives_extra = jnp.logical_or(half == 0, seq < 30)

    @pl.when(has_extra)
    def _():
        greet(sister, seq - 2 * (1 - half))

    @pl.when(section == 0)
    def _():
        for k in range(1, 8):
            greet(2 * k + half, seq)

    for f in range(CHUNKS):
        entering[0, f] = start_ref[0, 0, :, f * CHUNK:(f + 1) * CHUNK]

    one = jnp.int32(1)
    zero = jnp.int32(0)
    expected = (
        7 + 3 + jnp.where(section < 7, 8 * one, zero) + 8 - jnp.where(zrow == 0, one, zero)
        + jnp.where(seq < 31, one, zero) + jnp.where(gives_extra, one, zero)
        + jnp.where(section > 0, one, zero)
    )
    pl.semaphore_wait(barrier, expected)

    def near_copy(t, part):
        span = pl.ds(part * PER_PART, PER_PART)
        return remote(
            entering.at[t, span], halo.at[t, half, span], halo_send.at[0, part],
            halo_recv.at[t, 0, part], slot, seq + 1,
        )

    def forward_copy(t, part):
        span = pl.ds(part * PER_PART, PER_PART)
        return remote(
            halo.at[t, half, span], halo.at[t, half, span], halo_send.at[1, part],
            halo_recv.at[t, 1, part], sister, seq,
        )

    def forward_wait(t, part):
        span = pl.ds(part * PER_PART, PER_PART)
        return remote(
            halo.at[t, 1 - half, span], halo.at[t, 1 - half, span], halo_send.at[1, part],
            halo_recv.at[t, 1, part], sister, seq,
        )

    def extra_copy(t, part):
        span = pl.ds(part * PER_PART, PER_PART)
        return remote(
            entering.at[t, span], halo.at[t, 2, span], halo_send.at[2, part],
            halo_recv.at[t, 2, part], sister, seq + 2 * half,
        )

    def near_wait(t, part):
        span = pl.ds(part * PER_PART, PER_PART)
        return remote(
            entering.at[t, span], halo.at[t, half, span], halo_send.at[0, part],
            halo_recv.at[t, 0, part], slot, seq,
        )

    def send_halo(t, part):
        @pl.when(seq < 31)
        def _():
            near_copy(t, part).start()

        @pl.when(gives_extra)
        def _():
            extra_copy(t, part).start()

    param_copies = [
        remote(src, dst, param_send.at[k], param_recv.at[k], sister, seq)
        for k, (src, dst) in enumerate(param_pairs)
    ]
    weight_copies = [
        remote(ref.at[0], weights.at[k, place], weight_send.at[k], weight_recv.at[k], sister, seq)
        for k, ref in enumerate(weight_refs)
    ]
    other = pl.ds(pl.multiple_of((1 - half) * 512, 512), 512)
    fresh_copy = remote(
        fresh_ref.at[:, 0, 1 - half], fresh_in, fresh_send, fresh_recv, sister, seq
    )
    for copy in param_copies:
        copy.start()
    for part in range(HALO_PARTS):
        send_halo(0, part)
    for copy in weight_copies:
        copy.start()
    fresh_copy.start()

    row_num = lax.broadcasted_iota(jnp.int32, (ROWS, ROWS), 0)
    col_num = lax.broadcasted_iota(jnp.int32, (ROWS, ROWS), 1)
    pairing = pairing_ref[section]
    for layer in range(MIXES):
        back = jnp.where(row_num == pairing[layer:layer + 1, :], F32(1), F32(0))
        onehot[layer, 0] = back.T.astype(BF)
        onehot[layer, 1] = back.astype(BF)

    drop = jnp.full((ROWS, ROWS), -1e30, F32)
    keep = jnp.zeros((ROWS, ROWS), F32)
    for place_num, reach in ((0, 2 + half), (1, 1 + half), (2, 3 - 2 * half)):
        seen = table_ref[0, half, reach - 1]
        inside = jnp.where(2 * seq + half - reach >= 0, one, zero)
        shown = jnp.full((ROWS, ROWS), seen * inside, jnp.int32)
        flags = jnp.where(shown == 1, keep, drop)
        bias[0:ROWS, place_num * ROWS:(place_num + 1) * ROWS] = flags
        bias[ROWS:2 * ROWS, place_num * ROWS:(place_num + 1) * ROWS] = flags
    causal = jnp.where(col_num <= row_num, keep, drop)
    bias[0:ROWS, 3 * ROWS:] = causal
    bias[ROWS:2 * ROWS, 3 * ROWS:] = causal

    for copy in local_params:
        copy.wait()
    for k, (_, dst) in enumerate(
        ((None, gains.at[1 - half]), (None, angles.at[1 - half]), (None, scales.at[1 - half]))
    ):
        remote(dst, dst, param_send.at[k], param_recv.at[k], sister, seq).wait_recv()
    feature_half = mine // 4
    features = pl.ds(pl.multiple_of((mine % 4) * CHUNK, CHUNK), CHUNK)
    angle = angles[feature_half, :, features]
    cosine = jnp.cos(angle)
    sine = jnp.sin(angle)
    for layer in range(MIXES):
        scale = scales[feature_half, layer, :, features]
        c = cosine[layer:layer + 1]
        n = sine[layer:layer + 1]
        coef[layer, 0:1] = scale[0:1] * c
        coef[layer, 1:2] = scale[0:1] * n
        coef[layer, 2:3] = scale[1:2] * c
        coef[layer, 3:4] = scale[1:2] * n

    def norm(block, place_num):
        total = jnp.zeros((ROWS, 1), F32)
        for f in range(CHUNKS):
            wide = block[f].astype(F32)
            total = total + jnp.sum(wide * wide, axis=-1, keepdims=True)
        factor = lax.rsqrt(total * (1.0 / WIDE) + 1e-6)
        for f in range(CHUNKS):
            part = pl.ds((f % 4) * CHUNK, CHUNK)
            gain = gains[f // 4, :, part]
            normed[place_num * ROWS:(place_num + 1) * ROWS, f * CHUNK:(f + 1) * CHUNK] = (
                block[f].astype(F32) * factor * gain
            ).astype(BF)

    def project(which, rows, target, scale=None):
        def one_part(k, carry):
            cols = pl.ds(pl.multiple_of(k * 256, 256), 256)
            product = jnp.dot(
                normed[rows, :], weights[which, :, cols], preferred_element_type=F32
            )
            if scale is None:
                target[rows, cols] = product.astype(BF)
            else:
                target[:, cols] = (product * scale).astype(BF)
            return carry

        lax.fori_loop(0, 4, one_part, 0)

    def await_weight(t, which):
        @pl.when(t == 0)
        def _():
            local_weights[which].wait()
            remote(
                weights.at[which, other], weights.at[which, other], weight_send.at[which],
                weight_recv.at[which], sister, seq,
            ).wait_recv()

    def mix(layer, lower, upper):
        count = len(lower)
        low = jnp.concatenate(lower, axis=1)
        up = jnp.concatenate(upper, axis=1)
        rows = [
            jnp.concatenate([coef[layer, k:k + 1]] * count, axis=1) for k in range(4)
        ]
        to_low = jnp.dot(onehot[layer, 0], up, preferred_element_type=F32)
        to_up = jnp.dot(onehot[layer, 1], low, preferred_element_type=F32)
        new_low = (rows[0] * low.astype(F32) + rows[1] * to_low).astype(BF)
        new_up = (rows[2] * up.astype(F32) - rows[3] * to_up).astype(BF)
        cut = lambda whole: [whole[:, k * CHUNK:(k + 1) * CHUNK] for k in range(count)]
        return cut(new_low), cut(new_up)

    def mix_all(layer, bit, blocks):
        lows = [b for b in range(len(blocks)) if not b >> bit & 1]
        ups = [b | 1 << bit for b in lows]
        new_low, new_up = mix(layer, [blocks[b] for b in lows], [blocks[b] for b in ups])
        result = list(blocks)
        for k, b in enumerate(lows):
            result[b] = new_low[k]
        for k, b in enumerate(ups):
            result[b] = new_up[k]
        return result

    lane = lax.broadcasted_iota(jnp.int32, (1, CHUNK), 1)
    first_head = jnp.where(lane < 64, F32(1), F32(0))
    pick_first = first_head.astype(BF)
    pick_second = (1 - first_head).astype(BF)

    def tick(t, carry):
        for part in range(HALO_PARTS):
            @pl.when(t > 0)
            def _():
                for f in range(part * PER_PART, (part + 1) * PER_PART):
                    piece = remote(
                        entering.at[t, f], entering.at[t, f], back_send.at[0],
                        back_recv.at[t, f], slot, seq,
                    )
                    if f == 0:
                        @pl.when(section > 0)
                        def _():
                            piece.wait_recv()
                    else:
                        piece.wait_recv()
                send_halo(t, part)

        norm(entering.at[t], 3)
        own_rows = pl.ds(3 * ROWS, ROWS)
        await_weight(t, 0)
        project(0, own_rows, keys)
        await_weight(t, 1)
        project(1, own_rows, values)
        await_weight(t, 2)
        project(2, own_rows, queries, scale=0.125)

        @pl.when(t == 0)
        def _():
            fresh_copy.wait_recv()
            for k in range(TICKS - 1):
                own = fresh_ref[k, 0, half].astype(F32)
                theirs = fresh_in[k].astype(F32)
                even = jnp.concatenate([own, theirs], axis=1)
                odd = jnp.concatenate([theirs, own], axis=1)
                fresh_full[k] = jnp.where(half == 0, even, odd).astype(BF)

                @pl.when(section == 0)
                def _():
                    entering[k + 1, 0] = fresh_full[k]

                @pl.when(section > 0)
                def _():
                    remote(
                        fresh_full.at[k], entering.at[k + 1, section], full_send.at[k],
                        back_recv.at[k + 1, section], half, seq,
                    ).start()

        for part in range(HALO_PARTS):
            @pl.when(seq > 0)
            def _():
                near_wait(t, part).wait_recv()
                forward_copy(t, part).start()
        for part in range(HALO_PARTS):
            @pl.when(has_extra)
            def _():
                extra_copy(t, part).wait_recv()
        norm(halo.at[t, 2], 2)
        for part in range(HALO_PARTS):
            @pl.when(seq > 0)
            def _():
                forward_wait(t, part).wait_recv()
        norm(halo.at[t, 0], 0)
        norm(halo.at[t, 1], 1)
        near_rows = pl.ds(0, 3 * ROWS)
        project(0, near_rows, keys)
        project(1, near_rows, values)

        def two_heads(k, carry):
            cols = pl.ds(pl.multiple_of(k * CHUNK, CHUNK), CHUNK)
            both = queries[:, cols]
            stacked = jnp.concatenate([both * pick_first, both * pick_second], axis=0)
            scores = lax.dot_general(
                stacked, keys[:, cols], (((1,), (1,)), ((), ())), preferred_element_type=F32
            ) + bias[...]
            top = jnp.max(scores, axis=-1, keepdims=True)
            expo = jnp.exp(scores - top)
            total = jnp.sum(expo, axis=-1, keepdims=True)
            summed = jnp.dot(expo.astype(BF), values[:, cols], preferred_element_type=F32) / total
            attended[:, cols] = jnp.where(lane < 64, summed[:ROWS], summed[ROWS:]).astype(BF)
            return carry

        lax.fori_loop(0, CHUNKS, two_heads, 0)
        await_weight(t, 3)

        sends = []
        for away in (2, 1, 3, 0):
            target = (x + away) % 4
            cols = pl.ds(pl.multiple_of(target * 256, 256), 256)
            product = jnp.dot(attended[...], weights[3, :, cols], preferred_element_type=F32)
            for c in range(2):
                f = 2 * target + c
                mixed[f] = (
                    entering[t, f].astype(F32) + product[:, c * CHUNK:(c + 1) * CHUNK]
                ).astype(BF)
            if away:
                for c in range(2):
                    copy = remote(
                        mixed.at[2 * target + c], row_in.at[t, mine],
                        row_send.at[2 * away - 1 + c], row_recv.at[t, mine],
                        2 * section + c, 4 * z + target,
                    )
                    copy.start()
                    sends.append(copy)
            else:
                copy = remote(
                    mixed.at[2 * x + 1 - half], row_in.at[t, mine], row_send.at[0],
                    row_recv.at[t, mine], sister, seq,
                )
                copy.start()
                sends.append(copy)
        row_in[t, mine] = mixed[mine]
        for k in range(1, CHUNKS):
            source = (mine + k) % CHUNKS
            remote(
                row_in.at[t, source], row_in.at[t, source], row_send.at[0],
                row_recv.at[t, source], slot, seq,
            ).wait_recv()
        blocks = [row_in[t, b] for b in range(CHUNKS)]
        for layer in range(3):
            blocks = mix_all(layer, layer, blocks)
        for b in range(CHUNKS):
            row_out[b] = blocks[b]

        for k in (2, 1, 3):
            target = (zrow + k) % 4
            pair = (target + x) % 4
            copy = remote(
                row_out.at[pl.ds(2 * pair, 2)], col_in.at[t, zrow], col_send.at[k - 1],
                col_recv.at[t, zrow], slot, 4 * (zbase + target) + x,
            )
            copy.start()
            sends.append(copy)
        for c in range(2):
            col_in[t, zrow, c] = row_out[2 * held + c]
        for k in range(1, 4):
            source = (zrow + k) % 4
            remote(
                col_in.at[t, source], col_in.at[t, source], col_send.at[0],
                col_recv.at[t, source], slot, seq,
            ).wait_recv()
        blocks = [col_in[t, r, c] for r in range(4) for c in range(2)]
        for layer in range(3, MIXES):
            blocks = mix_all(layer, layer - 2, blocks)
        for b in range(CHUNKS):
            col_out[b] = blocks[b]

        ahead = jnp.where(t < TICKS - 1, one, zero)
        for k in range(4):
            target = (zrow + k) % 4
            for m in range(2):
                c = (half + m) % 2

                def back_copy():
                    return remote(
                        col_out.at[2 * target + c], entering.at[t + 1, mine],
                        back_send.at[2 * k + m], back_recv.at[t + 1, mine],
                        2 * (section + ahead) + c, 4 * (zbase + target) + held,
                    )

                if k == 0 and m == 0:
                    itself = jnp.logical_and(t == TICKS - 1, zrow == 0)

                    @pl.when(itself)
                    def _():
                        entering[t + 1, mine] = col_out[2 * target + c]

                    @pl.when(jnp.logical_and(
                        jnp.logical_not(itself), jnp.logical_or(t == TICKS - 1, section < 7)
                    ))
                    def _():
                        back_copy().start()
                else:
                    @pl.when(jnp.logical_or(t == TICKS - 1, section < 7))
                    def _():
                        back_copy().start()

        for copy in sends:
            copy.wait_send()
        for part in range(HALO_PARTS):
            @pl.when(seq < 31)
            def _():
                near_copy(t, part).wait_send()

            @pl.when(gives_extra)
            def _():
                extra_copy(t, part).wait_send()

            @pl.when(seq > 0)
            def _():
                forward_copy(t, part).wait_send()

        @pl.when(jnp.logical_or(t == TICKS - 1, section < 7))
        def _():
            for k in range(4):
                for m in range(2):
                    target = (zrow + k) % 4
                    c = (half + m) % 2
                    sent = remote(
                        col_out.at[2 * target + c], entering.at[t + 1, mine],
                        back_send.at[2 * k + m], back_recv.at[t + 1, mine],
                        slot, seq,
                    )
                    if k or m:
                        sent.wait_send()
                    else:
                        @pl.when(jnp.logical_or(t < TICKS - 1, zrow > 0))
                        def _():
                            sent.wait_send()

        @pl.when(t == 0)
        def _():
            for copy in param_copies + weight_copies + [fresh_copy]:
                copy.wait_send()

            @pl.when(section > 0)
            def _():
                for k in range(TICKS - 1):
                    remote(
                        fresh_full.at[k], entering.at[k + 1, section], full_send.at[k],
                        back_recv.at[k + 1, section], half, seq,
                    ).wait_send()

        return carry

    lax.fori_loop(0, TICKS, tick, 0)

    for f in range(CHUNKS):
        piece = remote(
            entering.at[TICKS, f], entering.at[TICKS, f], back_send.at[0],
            back_recv.at[TICKS, f], slot, seq,
        )

        @pl.when(jnp.logical_or(zrow > 0, mine != f))
        def _():
            piece.wait_recv()

        out_ref[0, 0, :, f * CHUNK:(f + 1) * CHUNK] = entering[TICKS, f]


def local(*args):
    dma = pltpu.SemaphoreType.DMA
    vmem = pl.BlockSpec(memory_space=pltpu.VMEM)
    hbm = pl.BlockSpec(memory_space=pl.ANY)
    smem = pl.BlockSpec(memory_space=pltpu.SMEM)
    block = (CHUNKS, ROWS, CHUNK)
    return pl.pallas_call(
        kernel,
        out_shape=jax.ShapeDtypeStruct((1, 1, ROWS, WIDE), BF),
        in_specs=[vmem, vmem, vmem, hbm, hbm, hbm, hbm, vmem, vmem, vmem, smem],
        out_specs=vmem,
        scratch_shapes=[
            pltpu.VMEM((4, WIDE, WIDE), BF),
            pltpu.VMEM((2, 1, 512), F32),
            pltpu.VMEM((2, MIXES, 512), F32),
            pltpu.VMEM((2, MIXES, 2, 512), F32),
            pltpu.VMEM((TICKS + 1,) + block, BF),
            pltpu.VMEM((TICKS, 3) + block, BF),
            pltpu.VMEM((4 * ROWS, WIDE), BF),
            pltpu.VMEM((ROWS, WIDE), BF),
            pltpu.VMEM((4 * ROWS, WIDE), BF),
            pltpu.VMEM((4 * ROWS, WIDE), BF),
            pltpu.VMEM((ROWS, WIDE), BF),
            pltpu.VMEM(block, BF),
            pltpu.VMEM((TICKS,) + block, BF),
            pltpu.VMEM(block, BF),
            pltpu.VMEM((TICKS, 4, 2, ROWS, CHUNK), BF),
            pltpu.VMEM(block, BF),
            pltpu.VMEM((MIXES, 2, ROWS, ROWS), BF),
            pltpu.VMEM((MIXES, 4, CHUNK), F32),
            pltpu.VMEM((2 * ROWS, 4 * ROWS), F32),
            pltpu.VMEM((TICKS - 1, ROWS, 64), BF),
            pltpu.VMEM((TICKS - 1, ROWS, CHUNK), BF),
            dma((4,)), dma((4,)), dma((4,)), dma((3,)), dma((3,)), dma((3,)),
            dma, dma, dma((TICKS - 1,)),
            dma((3, HALO_PARTS)), dma((TICKS, 3, HALO_PARTS)),
            dma((7,)), dma((TICKS, CHUNKS)),
            dma((3,)), dma((TICKS, 4)),
            dma((CHUNKS,)), dma((TICKS + 1, CHUNKS)),
        ],
        compiler_params=pltpu.CompilerParams(
            collective_id=0, has_side_effects=True, vmem_limit_bytes=48 * 1024 * 1024
        ),
    )(*args)


def solution(mesh):
    in_specs = (
        P("seq", "section", None, None),
        P(None, "seq", None, None, "section"),
        P("section", None),
        P("section", None, None),
        P("section", None, None),
        P("section", None, None),
        P("section", None, None),
        P("section", None, None),
        P("section", None, None, None),
        P(),
        P("seq", None, None),
    )
    out_specs = P("seq", "section", None, None)

    def run(start, fresh, gain, asking, lookup, content, emitting, turning, scaling, lines, table):
        return jax.shard_map(
            local, mesh=mesh, in_specs=in_specs, out_specs=out_specs, check_vma=False
        )(start, fresh, gain, asking, lookup, content, emitting, turning, scaling, lines, table)

    return run
```

time: 529 us -> 174 us (0.33)
  the two profiles are of different devices: /device:TPU:480 before, /device:TPU:481 now
where the time goes in v1:
time: 174 us; the launch traced here: 173 us
  Pallas kernels  164 us (94%)
  local copies, waits for them, and re-layouts  8.79 us (5%)
    pallas_call x1, Pallas kernels, local(): pl.pallas_call(kernel, out_shape=jax.ShapeDtypeStruct((1, 1, ROWS, WIDE),...  164 us
    unnamed x20, local copies, waits for them, and re-layouts  8.79 us

profile of v1, /device:TPU:481, one launch (start us, length us, event | category | flops | bytes accessed | tf_op | source)
XLA Modules:
  0.0 172.5 jit_solution(9673529910881738276)
XLA Ops:
  0.0 0.0 copy-start.4
  0.0 0.7 copy.13.angle_ref
  0.8 0.7 copy.14.pairing_ref
  1.5 0.0 copy-start.6
  1.5 0.0 copy-start.7
  1.5 1.0 copy.12.fresh_ref
  2.5 0.0 copy-done.4
  2.5 0.0 copy-done.6
  2.5 0.0 copy-done.7
  2.5 0.0 copy-start
  2.5 1.2 copy-done
  3.7 0.0 copy-start.1
  3.7 1.2 copy-done.1
  5.0 0.0 copy-start.2
  5.0 1.2 copy-done.2
  6.2 0.0 copy-start.3
  6.2 1.2 copy-done.3
  7.4 0.0 copy-start.5
  7.4 0.7 copy-done.5
  8.1 163.7 %shard_map.109 = bf16[1,1,128,1024]{3,2,1,0:T(8,128)(2,1)S(1)} custom-call(bf16[1,1,128,1024]{3,2,1,0:T(8,128)(2,1)S(1)} %copy-done.4, bf16[2,1,2,128,64]{4,3,2,1,0:T(8,128)(2,1)S(1)} %copy.12.fresh_ref, f32[1,512]{1,0:T(1,128)S(1)} %copy-done.6, bf16[1,512,1024]{2,1,0:T(8,128)(2,1)S(1)} %copy-done, bf16[1,512,1024]{2,1,0:T(8,128)(2,1)S(1)} %copy-done.1, ...), custom_call_target="tpu_custom_call" | custom-call | tf_op jit(solution)/shard_map/pallas_call | solution.py:548
  171.8 0.7 copy.16
Async XLA Ops:
  0.0 2.5 %copy-start.4 = (bf16[1,1,128,1024]{3,2,1,0:T(8,128)(2,1)S(1)}, bf16[1,1,128,1024]{3,2,1,0:T(8,128)(2,1)}, u32[]{:S(2)}) copy-start(bf16[1,1,128,1024]{3,2,1,0:T(8,128)(2,1)} %start_ref.1) | copy-start | bytes 786436
  1.5 1.0 copy-start.6
  1.5 1.0 copy-start.7
  2.5 1.2 copy-start
  3.7 1.2 copy-start.1
  5.0 1.2 copy-start.2
  6.2 1.2 copy-start.3
  7.4 0.7 copy-start.5

commit v2 on v1

--- a/solution.py
+++ b/solution.py
@@ -9,6 +9,7 @@
 WIN = 3
 MIXES = 5
 TICKS = 3
+FAR = 4
 ROWS = 128
 CHUNK = 128
 CHUNKS = 8
@@ -35,7 +36,9 @@
     pairing_ref, table_ref,
     out_ref,
     weights, gains, angles, scales, entering, halo, normed, queries, keys, values, attended,
-    mixed, row_in, row_out, col_in, col_out, onehot, coef, bias, fresh_in, fresh_full,
+    mixed, row_in, row_out, col_in, col_out, onehot, coef, bias, fresh_own, fresh_in, fresh_full,
+    pairing, relay,
+    start_sem, pairing_sem, fresh_sem, relay_send, relay_recv,
     weight_local, weight_send, weight_recv, param_local, param_send, param_recv,
     fresh_send, fresh_recv, full_send,
     halo_send, halo_recv, row_send, row_recv, col_send, col_recv, back_send, back_recv,
@@ -60,13 +63,21 @@
     ]
     param_pairs = (
         (gain_ref, gains.at[half]),
-        (angle_ref.at[0], angles.at[half]),
+        (angle_ref, angles.at[half]),
         (scale_ref.at[0], scales.at[half]),
     )
     local_params = [
         pltpu.make_async_copy(src, dst, param_local.at[k]) for k, (src, dst) in enumerate(param_pairs)
     ]
-    for copy in local_weights + local_params:
+    local_starts = [
+        pltpu.make_async_copy(
+            start_ref.at[0, 0, :, pl.ds(f * CHUNK, CHUNK)], entering.at[0, f], start_sem.at[f]
+        )
+        for f in range(CHUNKS)
+    ]
+    local_pairing = pltpu.make_async_copy(pairing_ref, pairing, pairing_sem)
+    local_fresh = pltpu.make_async_copy(fresh_ref.at[:, 0, half], fresh_own, fresh_sem)
+    for copy in local_starts + local_params + [local_pairing] + local_weights + [local_fresh]:
         copy.start()
 
     @pl.when(seq < 2)
@@ -90,7 +101,9 @@
         source = (mine + k) % CHUNKS
         source_seq = 4 * (zbase + (x - source // 2 + 4) % 4) + source // 2
 
-        @pl.when(section > 0)
+        @pl.when(jnp.logical_and(
+            section > 0, jnp.logical_or(section != FAR, source // 2 == 3)
+        ))
         def _():
             greet(2 * section - 2 + source % 2, source_seq)
 
@@ -117,15 +130,28 @@
         for k in range(1, 8):
             greet(2 * k + half, seq)
 
-    for f in range(CHUNKS):
-        entering[0, f] = start_ref[0, 0, :, f * CHUNK:(f + 1) * CHUNK]
+    relays = section < 3
+    relay_seq = 4 * (zbase + (x - section + 8) % 4) + section % 4
+
+    @pl.when(relays)
+    def _():
+        for c in range(2):
+            greet(2 * (FAR - 1) + c, relay_seq)
+
+    @pl.when(section == FAR)
+    def _():
+        for k in range(3):
+            greet(2 * k + half, seq)
+
+    for copy in local_starts:
+        copy.wait()
 
     one = jnp.int32(1)
     zero = jnp.int32(0)
     expected = (
         7 + 3 + jnp.where(section < 7, 8 * one, zero) + 8 - jnp.where(zrow == 0, one, zero)
         + jnp.where(seq < 31, one, zero) + jnp.where(gives_extra, one, zero)
-        + jnp.where(section > 0, one, zero)
+        + jnp.where(section > 0, one, zero) + jnp.where(relays, one, zero)
     )
     pl.semaphore_wait(barrier, expected)
 
@@ -195,9 +221,10 @@
 
     row_num = lax.broadcasted_iota(jnp.int32, (ROWS, ROWS), 0)
     col_num = lax.broadcasted_iota(jnp.int32, (ROWS, ROWS), 1)
-    pairing = pairing_ref[section]
+    local_pairing.wait()
     for layer in range(MIXES):
-        back = jnp.where(row_num == pairing[layer:layer + 1, :], F32(1), F32(0))
+        lines = pairing[layer, pl.ds(section, 1), :]
+        back = jnp.where(row_num == lines, F32(1), F32(0))
         onehot[layer, 0] = back.T.astype(BF)
         onehot[layer, 1] = back.astype(BF)
 
@@ -222,7 +249,7 @@
         remote(dst, dst, param_send.at[k], param_recv.at[k], sister, seq).wait_recv()
     feature_half = mine // 4
     features = pl.ds(pl.multiple_of((mine % 4) * CHUNK, CHUNK), CHUNK)
-    angle = angles[feature_half, :, features]
+    angle = angles[feature_half, :, 0, features]
     cosine = jnp.cos(angle)
     sine = jnp.sin(angle)
     for layer in range(MIXES):
@@ -328,13 +355,14 @@
 
         @pl.when(t == 0)
         def _():
+            local_fresh.wait()
             fresh_copy.wait_recv()
             for k in range(TICKS - 1):
-                own = fresh_ref[k, 0, half].astype(F32)
+                own = fresh_own[k].astype(F32)
                 theirs = fresh_in[k].astype(F32)
-                even = jnp.concatenate([own, theirs], axis=1)
-                odd = jnp.concatenate([theirs, own], axis=1)
-                fresh_full[k] = jnp.where(half == 0, even, odd).astype(BF)
+                even = jnp.concatenate([own, theirs], axis=0)
+                odd = jnp.concatenate([theirs, own], axis=0)
+                fresh_full[k] = jnp.where(half == 0, even, odd).T.astype(BF)
 
                 @pl.when(section == 0)
                 def _():
@@ -447,6 +475,11 @@
             col_out[b] = blocks[b]
 
         ahead = jnp.where(t < TICKS - 1, one, zero)
+        last = t == TICKS - 1
+        by_relay = jnp.logical_and(jnp.logical_and(section == FAR - 1, x < 3), t < TICKS - 1)
+        direct = jnp.logical_and(
+            jnp.logical_or(last, section < 7), jnp.logical_not(by_relay)
+        )
         for k in range(4):
             target = (zrow + k) % 4
             for m in range(2):
@@ -466,15 +499,38 @@
                     def _():
                         entering[t + 1, mine] = col_out[2 * target + c]
 
-                    @pl.when(jnp.logical_and(
-                        jnp.logical_not(itself), jnp.logical_or(t == TICKS - 1, section < 7)
-                    ))
+                    @pl.when(jnp.logical_and(jnp.logical_not(itself), direct))
                     def _():
                         back_copy().start()
                 else:
-                    @pl.when(jnp.logical_or(t == TICKS - 1, section < 7))
+                    @pl.when(direct)
                     def _():
                         back_copy().start()
+
+                @pl.when(by_relay)
+                def _():
+                    remote(
+                        col_out.at[2 * target + c], relay.at[t, half],
+                        back_send.at[2 * k + m], relay_recv.at[t, half],
+                        2 * x + c, 4 * (zbase + target) + held,
+                    ).start()
+
+        @pl.when(jnp.logical_and(relays, t < TICKS - 1))
+        def _():
+            for c in range(2):
+                remote(
+                    relay.at[t, c], relay.at[t, c], relay_send.at[c], relay_recv.at[t, c],
+                    slot, seq,
+                ).wait_recv()
+                remote(
+                    relay.at[t, c], entering.at[t + 1, 2 * section + c], relay_send.at[c],
+                    back_recv.at[t + 1, 2 * section + c], 2 * FAR + half, seq,
+                ).start()
+            for c in range(2):
+                remote(
+                    relay.at[t, c], relay.at[t, c], relay_send.at[c], relay_recv.at[t, c],
+                    slot, seq,
+                ).wait_send()
 
         for copy in sends:
             copy.wait_send()
@@ -542,18 +598,18 @@
 def local(*args):
     dma = pltpu.SemaphoreType.DMA
     vmem = pl.BlockSpec(memory_space=pltpu.VMEM)
-    hbm = pl.BlockSpec(memory_space=pl.ANY)
+    hbm = pl.BlockSpec(memory_space=pltpu.HBM)
     smem = pl.BlockSpec(memory_space=pltpu.SMEM)
     block = (CHUNKS, ROWS, CHUNK)
     return pl.pallas_call(
         kernel,
         out_shape=jax.ShapeDtypeStruct((1, 1, ROWS, WIDE), BF),
-        in_specs=[vmem, vmem, vmem, hbm, hbm, hbm, hbm, vmem, vmem, vmem, smem],
+        in_specs=[hbm] * 10 + [smem],
         out_specs=vmem,
         scratch_shapes=[
             pltpu.VMEM((4, WIDE, WIDE), BF),
             pltpu.VMEM((2, 1, 512), F32),
-            pltpu.VMEM((2, MIXES, 512), F32),
+            pltpu.VMEM((2, MIXES, 1, 512), F32),
             pltpu.VMEM((2, MIXES, 2, 512), F32),
             pltpu.VMEM((TICKS + 1,) + block, BF),
             pltpu.VMEM((TICKS, 3) + block, BF),
@@ -570,8 +626,12 @@
             pltpu.VMEM((MIXES, 2, ROWS, ROWS), BF),
             pltpu.VMEM((MIXES, 4, CHUNK), F32),
             pltpu.VMEM((2 * ROWS, 4 * ROWS), F32),
-            pltpu.VMEM((TICKS - 1, ROWS, 64), BF),
+            pltpu.VMEM((TICKS - 1, 64, ROWS), BF),
+            pltpu.VMEM((TICKS - 1, 64, ROWS), BF),
             pltpu.VMEM((TICKS - 1, ROWS, CHUNK), BF),
+            pltpu.VMEM((MIXES, 8, ROWS), jnp.int32),
+            pltpu.VMEM((TICKS - 1, 2, ROWS, CHUNK), BF),
+            dma((CHUNKS,)), dma, dma, dma((2,)), dma((TICKS - 1, 2)),
             dma((4,)), dma((4,)), dma((4,)), dma((3,)), dma((3,)), dma((3,)),
             dma, dma, dma((TICKS - 1,)),
             dma((3, HALO_PARTS)), dma((TICKS, 3, HALO_PARTS)),
@@ -580,7 +640,7 @@
             dma((CHUNKS,)), dma((TICKS + 1, CHUNKS)),
         ],
         compiler_params=pltpu.CompilerParams(
-            collective_id=0, has_side_effects=True, vmem_limit_bytes=48 * 1024 * 1024
+            collective_id=0, has_side_effects=True, vmem_limit_bytes=60 * 1024 * 1024
         ),
     )(*args)
 
@@ -588,13 +648,13 @@
 def solution(mesh):
     in_specs = (
         P("seq", "section", None, None),
-        P(None, "seq", None, None, "section"),
+        P(None, "seq", None, "section", None),
         P("section", None),
         P("section", None, None),
         P("section", None, None),
         P("section", None, None),
         P("section", None, None),
-        P("section", None, None),
+        P(None, "section", None),
         P("section", None, None, None),
         P(),
         P("seq", None, None),
@@ -604,6 +664,9 @@
     def run(start, fresh, gain, asking, lookup, content, emitting, turning, scaling, lines, table):
         return jax.shard_map(
             local, mesh=mesh, in_specs=in_specs, out_specs=out_specs, check_vma=False
-        )(start, fresh, gain, asking, lookup, content, emitting, turning, scaling, lines, table)
+        )(
+            start, jnp.swapaxes(fresh, 3, 4), gain, asking, lookup, content, emitting,
+            jnp.swapaxes(turning, 0, 1), scaling, jnp.swapaxes(lines, 0, 1), table,
+        )
 
     return run

time: 174 us -> 162 us (0.931)
  local copies, waits for them, and re-layouts: 8.79 us -> 1.67 us
  Pallas kernels: 164 us -> 158 us
    unnamed x20 -> x1, local copies, waits for them, and re-layouts: 8.79 us -> 1.67 us
    pallas_call x1, Pallas kernels: 164 us -> 158 us  [local(): pl.pallas_call(kernel, out_shape=jax.ShapeDtypeStruct((1, 1, ROWS, WIDE),...]
where the time goes in v2:
time: 162 us; the launch traced here: 160 us
  Pallas kernels  158 us (98%)
  local copies, waits for them, and re-layouts  1.67 us (1%)
    pallas_call x1, Pallas kernels, local(): pl.pallas_call(kernel, out_shape=jax.ShapeDtypeStruct((1, 1, ROWS, WIDE),...  158 us

profile of v2, /device:TPU:481, one launch (start us, length us, event | category | flops | bytes accessed | tf_op | source)
XLA Modules:
  0.0 159.6 jit_solution(3126474631434624166)
XLA Ops:
  0.0 157.9 %shard_map.109 = bf16[1,1,128,1024]{3,2,1,0:T(8,128)(2,1)} custom-call(bf16[1,1,128,1024]{3,2,1,0:T(8,128)(2,1)} %start_ref.1, bf16[2,1,2,64,128]{4,3,2,1,0:T(8,128)(2,1)} %bitcast.3, f32[1,512]{1,0:T(1,128)} %gain_ref.1, bf16[1,512,1024]{2,1,0:T(8,128)(2,1)} %wq_ref.1, bf16[1,512,1024]{2,1,0:T(8,128)(2,1)} %wk_ref.1, bf16[1,512,1024]{2,1,0:T(8,128)(2,1)} %wv_ref.1, ...), custom_call_target="tpu_custom_call" | custom-call | tf_op jit(solution)/shard_map/pallas_call | solution.py:604
  157.9 1.7 %copy.13 = bf16[1,1,128,1024]{3,2,1,0:T(8,128)(2,1)} copy(bf16[1,1,128,1024]{3,2,1,0:T(8,128)(2,1)} %shard_map.109) | data formatting | bytes 524288

commit v3 on v2

--- a/solution.py
+++ b/solution.py
@@ -14,7 +14,7 @@
 CHUNK = 128
 CHUNKS = 8
 WIDE = 1024
-HALO_PARTS = 2
+HALO_PARTS = 4
 PER_PART = CHUNKS // HALO_PARTS
 BF = jnp.bfloat16
 F32 = jnp.float32
@@ -41,7 +41,7 @@
     start_sem, pairing_sem, fresh_sem, relay_send, relay_recv,
     weight_local, weight_send, weight_recv, param_local, param_send, param_recv,
     fresh_send, fresh_recv, full_send,
-    halo_send, halo_recv, row_send, row_recv, col_send, col_recv, back_send, back_recv,
+    near_send, near_recv, ahead_send, halo_send, halo_recv, row_send, row_recv, col_send, col_recv, back_send, back_recv,
 ):
     slot = lax.axis_index("section")
     seq = lax.axis_index("seq")
@@ -118,6 +118,16 @@
     def _():
         greet(slot, seq - 1)
 
+    fed = jnp.logical_and(section != 0, section != FAR)
+    feeds = jnp.logical_and(section != 7, section != FAR - 1)
+    before = jnp.maximum(seq - 1, 0)
+
+    @pl.when(jnp.logical_and(fed, seq > 0))
+    def _():
+        for f in range(CHUNKS):
+            row = (before % 4 - f // 2 + 4) % 4
+            greet(2 * section - 2 + f % 2, 4 * (before // 16 * 4 + row) + f // 2)
+
     has_extra = jnp.logical_or(half == 1, seq >= 2)
     gives_extra = jnp.logical_or(half == 0, seq < 30)
 
@@ -152,48 +162,53 @@
         7 + 3 + jnp.where(section < 7, 8 * one, zero) + 8 - jnp.where(zrow == 0, one, zero)
         + jnp.where(seq < 31, one, zero) + jnp.where(gives_extra, one, zero)
         + jnp.where(section > 0, one, zero) + jnp.where(relays, one, zero)
+        + jnp.where(feeds, 8 * one, zero)
+        - jnp.where(
+            jnp.logical_and(feeds, jnp.logical_and(held == 3, zbase == 4)), 2 * one, zero
+        )
     )
     pl.semaphore_wait(barrier, expected)
 
-    def near_copy(t, part):
-        span = pl.ds(part * PER_PART, PER_PART)
+    def near_copy(t, f, to_seq):
         return remote(
-            entering.at[t, span], halo.at[t, half, span], halo_send.at[0, part],
-            halo_recv.at[t, 0, part], slot, seq + 1,
-        )
+            entering.at[t, f], halo.at[t, half, f], near_send.at[f], near_recv.at[t, f],
+            slot, to_seq,
+        )
+
+    def by_neighbor(t):
+        return jnp.logical_or(t == 0, jnp.logical_not(fed))
 
     def forward_copy(t, part):
-        span = pl.ds(part * PER_PART, PER_PART)
+        span = pl.ds(PER_PART * part, PER_PART)
         return remote(
             halo.at[t, half, span], halo.at[t, half, span], halo_send.at[1, part],
             halo_recv.at[t, 1, part], sister, seq,
         )
 
     def forward_wait(t, part):
-        span = pl.ds(part * PER_PART, PER_PART)
+        span = pl.ds(PER_PART * part, PER_PART)
         return remote(
             halo.at[t, 1 - half, span], halo.at[t, 1 - half, span], halo_send.at[1, part],
             halo_recv.at[t, 1, part], sister, seq,
         )
 
     def extra_copy(t, part):
-        span = pl.ds(part * PER_PART, PER_PART)
+        span = pl.ds(PER_PART * part, PER_PART)
         return remote(
             entering.at[t, span], halo.at[t, 2, span], halo_send.at[2, part],
             halo_recv.at[t, 2, part], sister, seq + 2 * half,
         )
 
-    def near_wait(t, part):
-        span = pl.ds(part * PER_PART, PER_PART)
+    def relay_wait(t, c):
         return remote(
-            entering.at[t, span], halo.at[t, half, span], halo_send.at[0, part],
-            halo_recv.at[t, 0, part], slot, seq,
+            relay.at[t, c], relay.at[t, c], relay_send.at[t, c], relay_recv.at[t, c], slot, seq
         )
 
     def send_halo(t, part):
-        @pl.when(seq < 31)
-        def _():
-            near_copy(t, part).start()
+        @pl.when(jnp.logical_and(seq < 31, by_neighbor(t)))
+        def _():
+            for c in range(PER_PART):
+                near_copy(t, PER_PART * part + c, seq + 1).start()
 
         @pl.when(gives_extra)
         def _():
@@ -286,7 +301,7 @@
                 target[:, cols] = (product * scale).astype(BF)
             return carry
 
-        lax.fori_loop(0, 4, one_part, 0)
+        lax.fori_loop(0, 4, one_part, 0, unroll=4)
 
     def await_weight(t, which):
         @pl.when(t == 0)
@@ -327,17 +342,58 @@
     pick_first = first_head.astype(BF)
     pick_second = (1 - first_head).astype(BF)
 
+    def ahead_copy(t, k, m):
+        target = (zrow + k) % 4
+        c = (half + m) % 2
+        pair = 4 * (zbase + target) + held
+        return pair, remote(
+            col_out.at[2 * target + c], halo.at[t + 1, c, mine], ahead_send.at[2 * k + m],
+            near_recv.at[t + 1, mine], 2 * section + 2 + c, jnp.minimum(pair + 1, 31),
+        )
+
+    def back_sent(t):
+        @pl.when(jnp.logical_or(t == TICKS - 1, section < 7))
+        def _():
+            for k in range(4):
+                for m in range(2):
+                    target = (zrow + k) % 4
+                    c = (half + m) % 2
+                    sent = remote(
+                        col_out.at[2 * target + c], entering.at[t + 1, mine],
+                        back_send.at[2 * k + m], back_recv.at[t + 1, mine],
+                        slot, seq,
+                    )
+                    if k or m:
+                        sent.wait_send()
+                    else:
+                        @pl.when(jnp.logical_or(t < TICKS - 1, zrow > 0))
+                        def _():
+                            sent.wait_send()
+
+        @pl.when(jnp.logical_and(feeds, t < TICKS - 1))
+        def _():
+            for k in range(4):
+                for m in range(2):
+                    pair, copy_ahead = ahead_copy(t, k, m)
+
+                    @pl.when(pair < 31)
+                    def _():
+                        copy_ahead.wait_send()
+
     def tick(t, carry):
-        for part in range(HALO_PARTS):
+        for step in range(HALO_PARTS):
+            part = (x - zrow + step + 4) % 4
+
             @pl.when(t > 0)
             def _():
-                for f in range(part * PER_PART, (part + 1) * PER_PART):
+                for c in range(PER_PART):
+                    f = PER_PART * part + c
                     piece = remote(
                         entering.at[t, f], entering.at[t, f], back_send.at[0],
                         back_recv.at[t, f], slot, seq,
                     )
-                    if f == 0:
-                        @pl.when(section > 0)
+                    if c == 0:
+                        @pl.when(jnp.logical_or(section > 0, part > 0))
                         def _():
                             piece.wait_recv()
                     else:
@@ -375,10 +431,13 @@
                         back_recv.at[k + 1, section], half, seq,
                     ).start()
 
-        for part in range(HALO_PARTS):
+        for step in range(HALO_PARTS):
+            part = (before % 4 - before // 4 % 4 + step + 4) % 4
+
             @pl.when(seq > 0)
             def _():
-                near_wait(t, part).wait_recv()
+                for c in range(PER_PART):
+                    near_copy(t, PER_PART * part + c, seq).wait_recv()
                 forward_copy(t, part).start()
         for part in range(HALO_PARTS):
             @pl.when(has_extra)
@@ -409,8 +468,12 @@
             attended[:, cols] = jnp.where(lane < 64, summed[:ROWS], summed[ROWS:]).astype(BF)
             return carry
 
-        lax.fori_loop(0, CHUNKS, two_heads, 0)
+        lax.fori_loop(0, CHUNKS, two_heads, 0, unroll=4)
         await_weight(t, 3)
+
+        @pl.when(t > 0)
+        def _():
+            back_sent(t - 1)
 
         sends = []
         for away in (2, 1, 3, 0):
@@ -515,29 +578,32 @@
                         2 * x + c, 4 * (zbase + target) + held,
                     ).start()
 
+        @pl.when(jnp.logical_and(feeds, t < TICKS - 1))
+        def _():
+            for k in range(4):
+                for m in range(2):
+                    pair, copy_ahead = ahead_copy(t, k, m)
+
+                    @pl.when(pair < 31)
+                    def _():
+                        copy_ahead.start()
+
         @pl.when(jnp.logical_and(relays, t < TICKS - 1))
         def _():
             for c in range(2):
+                relay_wait(t, c).wait_recv()
                 remote(
-                    relay.at[t, c], relay.at[t, c], relay_send.at[c], relay_recv.at[t, c],
-                    slot, seq,
-                ).wait_recv()
-                remote(
-                    relay.at[t, c], entering.at[t + 1, 2 * section + c], relay_send.at[c],
+                    relay.at[t, c], entering.at[t + 1, 2 * section + c], relay_send.at[t, c],
                     back_recv.at[t + 1, 2 * section + c], 2 * FAR + half, seq,
                 ).start()
-            for c in range(2):
-                remote(
-                    relay.at[t, c], relay.at[t, c], relay_send.at[c], relay_recv.at[t, c],
-                    slot, seq,
-                ).wait_send()
 
         for copy in sends:
             copy.wait_send()
         for part in range(HALO_PARTS):
-            @pl.when(seq < 31)
-            def _():
-                near_copy(t, part).wait_send()
+            @pl.when(jnp.logical_and(seq < 31, by_neighbor(t)))
+            def _():
+                for c in range(PER_PART):
+                    near_copy(t, PER_PART * part + c, seq + 1).wait_send()
 
             @pl.when(gives_extra)
             def _():
@@ -546,24 +612,6 @@
             @pl.when(seq > 0)
             def _():
                 forward_copy(t, part).wait_send()
-
-        @pl.when(jnp.logical_or(t == TICKS - 1, section < 7))
-        def _():
-            for k in range(4):
-                for m in range(2):
-                    target = (zrow + k) % 4
-                    c = (half + m) % 2
-                    sent = remote(
-                        col_out.at[2 * target + c], entering.at[t + 1, mine],
-                        back_send.at[2 * k + m], back_recv.at[t + 1, mine],
-                        slot, seq,
-                    )
-                    if k or m:
-                        sent.wait_send()
-                    else:
-                        @pl.when(jnp.logical_or(t < TICKS - 1, zrow > 0))
-                        def _():
-                            sent.wait_send()
 
         @pl.when(t == 0)
         def _():
@@ -581,6 +629,13 @@
         return carry
 
     lax.fori_loop(0, TICKS, tick, 0)
+    back_sent(TICKS - 1)
+
+    @pl.when(relays)
+    def _():
+        for t in range(TICKS - 1):
+            for c in range(2):
+                relay_wait(t, c).wait_send()
 
     for f in range(CHUNKS):
         piece = remote(
@@ -631,9 +686,10 @@
             pltpu.VMEM((TICKS - 1, ROWS, CHUNK), BF),
             pltpu.VMEM((MIXES, 8, ROWS), jnp.int32),
             pltpu.VMEM((TICKS - 1, 2, ROWS, CHUNK), BF),
-            dma((CHUNKS,)), dma, dma, dma((2,)), dma((TICKS - 1, 2)),
+            dma((CHUNKS,)), dma, dma, dma((TICKS - 1, 2)), dma((TICKS - 1, 2)),
             dma((4,)), dma((4,)), dma((4,)), dma((3,)), dma((3,)), dma((3,)),
             dma, dma, dma((TICKS - 1,)),
+            dma((CHUNKS,)), dma((TICKS, CHUNKS)), dma((CHUNKS,)),
             dma((3, HALO_PARTS)), dma((TICKS, 3, HALO_PARTS)),
             dma((7,)), dma((TICKS, CHUNKS)),
             dma((3,)), dma((TICKS, 4)),

time: 162 us -> 151 us (0.932)
  the two profiles are of different devices: /device:TPU:481 before, /device:TPU:353 now
where the time goes in v3:
time: 151 us
  Pallas kernels  149 us (99%)
  local copies, waits for them, and re-layouts  1.67 us (1%)
    pallas_call x1, Pallas kernels, local(): pl.pallas_call(kernel, out_shape=jax.ShapeDtypeStruct((1, 1, ROWS, WIDE),...  149 us

profile of v3, /device:TPU:353, one launch (start us, length us, event | category | flops | bytes accessed | tf_op | source)
XLA Modules:
  0.0 150.7 jit_solution(10421732169834076443)
XLA Ops:
  0.0 149.0 %shard_map.109 = bf16[1,1,128,1024]{3,2,1,0:T(8,128)(2,1)} custom-call(bf16[1,1,128,1024]{3,2,1,0:T(8,128)(2,1)} %start_ref.1, bf16[2,1,2,64,128]{4,3,2,1,0:T(8,128)(2,1)} %bitcast.3, f32[1,512]{1,0:T(1,128)} %gain_ref.1, bf16[1,512,1024]{2,1,0:T(8,128)(2,1)} %wq_ref.1, bf16[1,512,1024]{2,1,0:T(8,128)(2,1)} %wk_ref.1, bf16[1,512,1024]{2,1,0:T(8,128)(2,1)} %wv_ref.1, ...), custom_call_target="tpu_custom_call" | custom-call | tf_op jit(solution)/shard_map/pallas_call | solution.py:659
  149.0 1.7 %copy.13 = bf16[1,1,128,1024]{3,2,1,0:T(8,128)(2,1)} copy(bf16[1,1,128,1024]{3,2,1,0:T(8,128)(2,1)} %shard_map.109) | data formatting | bytes 524288

commit v4 on v3

--- a/solution.py
+++ b/solution.py
@@ -37,7 +37,7 @@
     out_ref,
     weights, gains, angles, scales, entering, halo, normed, queries, keys, values, attended,
     mixed, row_in, row_out, col_in, col_out, onehot, coef, bias, fresh_own, fresh_in, fresh_full,
-    pairing, relay,
+    pairing, relay, ready,
     start_sem, pairing_sem, fresh_sem, relay_send, relay_recv,
     weight_local, weight_send, weight_recv, param_local, param_send, param_recv,
     fresh_send, fresh_recv, full_send,
@@ -101,9 +101,7 @@
         source = (mine + k) % CHUNKS
         source_seq = 4 * (zbase + (x - source // 2 + 4) % 4) + source // 2
 
-        @pl.when(jnp.logical_and(
-            section > 0, jnp.logical_or(section != FAR, source // 2 == 3)
-        ))
+        @pl.when(jnp.logical_and(section > 0, section != FAR))
         def _():
             greet(2 * section - 2 + source % 2, source_seq)
 
@@ -119,6 +117,7 @@
         greet(slot, seq - 1)
 
     fed = jnp.logical_and(section != 0, section != FAR)
+    crosses = jnp.logical_and(section == FAR - 1, x == 3)
     feeds = jnp.logical_and(section != 7, section != FAR - 1)
     before = jnp.maximum(seq - 1, 0)
 
@@ -148,26 +147,47 @@
         for c in range(2):
             greet(2 * (FAR - 1) + c, relay_seq)
 
-    @pl.when(section == FAR)
-    def _():
-        for k in range(3):
-            greet(2 * k + half, seq)
+    @pl.when(relays)
+    def _():
+        greet(2 * FAR + half, seq)
+
+    @pl.when(crosses)
+    def _():
+        for r in range(4):
+            pair = 4 * (zbase + r) + held
+            for c in range(2):
+                greet(2 * FAR + c, pair)
 
     for copy in local_starts:
         copy.wait()
 
     one = jnp.int32(1)
     zero = jnp.int32(0)
+    at_end = jnp.logical_and(held == 3, zbase == 4)
     expected = (
-        7 + 3 + jnp.where(section < 7, 8 * one, zero) + 8 - jnp.where(zrow == 0, one, zero)
+        7 + 3 + jnp.where(
+            jnp.logical_and(section < 7, jnp.logical_not(crosses)), 8 * one, zero
+        ) + 8 - jnp.where(zrow == 0, one, zero)
         + jnp.where(seq < 31, one, zero) + jnp.where(gives_extra, one, zero)
-        + jnp.where(section > 0, one, zero) + jnp.where(relays, one, zero)
+        + jnp.where(section > 0, one, zero)
+        + jnp.where(section == FAR, 5 * one, zero)
         + jnp.where(feeds, 8 * one, zero)
-        - jnp.where(
-            jnp.logical_and(feeds, jnp.logical_and(held == 3, zbase == 4)), 2 * one, zero
-        )
+        - jnp.where(jnp.logical_and(feeds, at_end), 2 * one, zero)
     )
     pl.semaphore_wait(barrier, expected)
+
+    def answer(to_section, to_seq):
+        pl.semaphore_signal(
+            ready, inc=1, device_id={"section": to_section, "seq": to_seq},
+            device_id_type=pl.DeviceIdType.MESH,
+        )
+
+    @pl.when(section == FAR)
+    def _():
+        for k in range(3):
+            answer(2 * k + half, seq)
+        for c in range(2):
+            answer(2 * (FAR - 1) + c, 4 * (zbase + (x + 1) % 4) + 3)
 
     def near_copy(t, f, to_seq):
         return remote(
@@ -198,6 +218,17 @@
             entering.at[t, span], halo.at[t, 2, span], halo_send.at[2, part],
             halo_recv.at[t, 2, part], sister, seq + 2 * half,
         )
+
+    def relay_copy(t, c):
+        return remote(
+            relay.at[t, c], entering.at[t + 1, 2 * section + c], relay_send.at[t, c],
+            back_recv.at[t + 1, 2 * section + c], 2 * FAR + half, seq,
+        )
+
+    def enter_wait(t, f):
+        remote(
+            entering.at[t, f], entering.at[t, f], back_send.at[0], back_recv.at[t, f], slot, seq
+        ).wait_recv()
 
     def relay_wait(t, c):
         return remote(
@@ -384,20 +415,10 @@
         for step in range(HALO_PARTS):
             part = (x - zrow + step + 4) % 4
 
-            @pl.when(t > 0)
+            @pl.when(jnp.logical_and(t > 0, section > 0))
             def _():
                 for c in range(PER_PART):
-                    f = PER_PART * part + c
-                    piece = remote(
-                        entering.at[t, f], entering.at[t, f], back_send.at[0],
-                        back_recv.at[t, f], slot, seq,
-                    )
-                    if c == 0:
-                        @pl.when(jnp.logical_or(section > 0, part > 0))
-                        def _():
-                            piece.wait_recv()
-                    else:
-                        piece.wait_recv()
+                    enter_wait(t, PER_PART * part + c)
                 send_halo(t, part)
 
         norm(entering.at[t], 3)
@@ -543,6 +564,10 @@
         direct = jnp.logical_and(
             jnp.logical_or(last, section < 7), jnp.logical_not(by_relay)
         )
+        @pl.when(jnp.logical_and(crosses, t == 0))
+        def _():
+            pl.semaphore_wait(ready, 8)
+
         for k in range(4):
             target = (zrow + k) % 4
             for m in range(2):
@@ -588,30 +613,40 @@
                     def _():
                         copy_ahead.start()
 
+        for part in range(HALO_PARTS):
+            @pl.when(jnp.logical_and(seq < 31, by_neighbor(t)))
+            def _():
+                for c in range(PER_PART):
+                    near_copy(t, PER_PART * part + c, seq + 1).wait_send()
+
+            @pl.when(gives_extra)
+            def _():
+                extra_copy(t, part).wait_send()
+
+            @pl.when(seq > 0)
+            def _():
+                forward_copy(t, part).wait_send()
+
+        @pl.when(jnp.logical_and(section == 0, t < TICKS - 1))
+        def _():
+            for part in range(HALO_PARTS):
+                for c in range(PER_PART):
+                    if part or c:
+                        enter_wait(t + 1, PER_PART * part + c)
+                send_halo(t + 1, part)
+
         @pl.when(jnp.logical_and(relays, t < TICKS - 1))
         def _():
+            @pl.when(t == 0)
+            def _():
+                pl.semaphore_wait(ready, 1)
+
             for c in range(2):
                 relay_wait(t, c).wait_recv()
-                remote(
-                    relay.at[t, c], entering.at[t + 1, 2 * section + c], relay_send.at[t, c],
-                    back_recv.at[t + 1, 2 * section + c], 2 * FAR + half, seq,
-                ).start()
+                relay_copy(t, c).start()
 
         for copy in sends:
             copy.wait_send()
-        for part in range(HALO_PARTS):
-            @pl.when(jnp.logical_and(seq < 31, by_neighbor(t)))
-            def _():
-                for c in range(PER_PART):
-                    near_copy(t, PER_PART * part + c, seq + 1).wait_send()
-
-            @pl.when(gives_extra)
-            def _():
-                extra_copy(t, part).wait_send()
-
-            @pl.when(seq > 0)
-            def _():
-                forward_copy(t, part).wait_send()
 
         @pl.when(t == 0)
         def _():
@@ -635,7 +670,7 @@
     def _():
         for t in range(TICKS - 1):
             for c in range(2):
-                relay_wait(t, c).wait_send()
+                relay_copy(t, c).wait_send()
 
     for f in range(CHUNKS):
         piece = remote(
@@ -686,6 +721,7 @@
             pltpu.VMEM((TICKS - 1, ROWS, CHUNK), BF),
             pltpu.VMEM((MIXES, 8, ROWS), jnp.int32),
             pltpu.VMEM((TICKS - 1, 2, ROWS, CHUNK), BF),
+            pltpu.SemaphoreType.REGULAR,
             dma((CHUNKS,)), dma, dma, dma((TICKS - 1, 2)), dma((TICKS - 1, 2)),
             dma((4,)), dma((4,)), dma((4,)), dma((3,)), dma((3,)), dma((3,)),
             dma, dma, dma((TICKS - 1,)),

time: 151 us -> 144 us (0.954)
  the two profiles are of different devices: /device:TPU:353 before, /device:TPU:481 now
where the time goes in v4:
time: 144 us; the launch traced here: 143 us
  Pallas kernels  142 us (99%)
  local copies, waits for them, and re-layouts  1.67 us (1%)
    pallas_call x1, Pallas kernels, local(): pl.pallas_call(kernel, out_shape=jax.ShapeDtypeStruct((1, 1, ROWS, WIDE),...  142 us

profile of v4, /device:TPU:481, one launch (start us, length us, event | category | flops | bytes accessed | tf_op | source)
XLA Modules:
  0.0 143.5 jit_solution(13039670945121178778)
XLA Ops:
  0.0 141.8 %shard_map.109 = bf16[1,1,128,1024]{3,2,1,0:T(8,128)(2,1)} custom-call(bf16[1,1,128,1024]{3,2,1,0:T(8,128)(2,1)} %start_ref.1, bf16[2,1,2,64,128]{4,3,2,1,0:T(8,128)(2,1)} %bitcast.3, f32[1,512]{1,0:T(1,128)} %gain_ref.1, bf16[1,512,1024]{2,1,0:T(8,128)(2,1)} %wq_ref.1, bf16[1,512,1024]{2,1,0:T(8,128)(2,1)} %wk_ref.1, bf16[1,512,1024]{2,1,0:T(8,128)(2,1)} %wv_ref.1, ...), custom_call_target="tpu_custom_call" | custom-call | tf_op jit(solution)/shard_map/pallas_call | solution.py:694
  141.8 1.7 %copy.13 = bf16[1,1,128,1024]{3,2,1,0:T(8,128)(2,1)} copy(bf16[1,1,128,1024]{3,2,1,0:T(8,128)(2,1)} %shard_map.109) | data formatting | bytes 524288

commit v5 on v4

--- a/solution.py
+++ b/solution.py
@@ -36,7 +36,7 @@
     pairing_ref, table_ref,
     out_ref,
     weights, gains, angles, scales, entering, halo, normed, queries, keys, values, attended,
-    mixed, row_in, row_out, col_in, col_out, onehot, coef, bias, fresh_own, fresh_in, fresh_full,
+    mixed, row_in, row_out, col_in, col_out, onehot, coef, earlier, bias, fresh_own, fresh_in, fresh_full,
     pairing, relay, ready,
     start_sem, pairing_sem, fresh_sem, relay_send, relay_recv,
     weight_local, weight_send, weight_recv, param_local, param_send, param_recv,
@@ -80,10 +80,6 @@
     for copy in local_starts + local_params + [local_pairing] + local_weights + [local_fresh]:
         copy.start()
 
-    @pl.when(seq < 2)
-    def _():
-        halo[...] = jnp.zeros_like(halo)
-
     barrier = pltpu.get_barrier_semaphore()
 
     def greet(to_section, to_seq):
@@ -157,6 +153,19 @@
             pair = 4 * (zbase + r) + held
             for c in range(2):
                 greet(2 * FAR + c, pair)
+
+    blank = jnp.zeros((CHUNKS, ROWS, CHUNK), BF)
+
+    @pl.when(seq == 0)
+    def _():
+        for t in range(TICKS):
+            halo[t, 0] = blank
+            halo[t, 1] = blank
+
+    @pl.when(jnp.logical_not(has_extra))
+    def _():
+        for t in range(TICKS):
+            halo[t, 2] = blank
 
     for copy in local_starts:
         copy.wait()
@@ -274,18 +283,16 @@
         onehot[layer, 0] = back.T.astype(BF)
         onehot[layer, 1] = back.astype(BF)
 
-    drop = jnp.full((ROWS, ROWS), -1e30, F32)
-    keep = jnp.zeros((ROWS, ROWS), F32)
-    for place_num, reach in ((0, 2 + half), (1, 1 + half), (2, 3 - 2 * half)):
+    drop = jnp.full((1, ROWS), -1e30, F32)
+    keep = jnp.zeros((1, ROWS), F32)
+    for place_num, reach in ((0, 1 + 2 * half), (1, 2), (2, 3 - 2 * half)):
         seen = table_ref[0, half, reach - 1]
         inside = jnp.where(2 * seq + half - reach >= 0, one, zero)
-        shown = jnp.full((ROWS, ROWS), seen * inside, jnp.int32)
-        flags = jnp.where(shown == 1, keep, drop)
-        bias[0:ROWS, place_num * ROWS:(place_num + 1) * ROWS] = flags
-        bias[ROWS:2 * ROWS, place_num * ROWS:(place_num + 1) * ROWS] = flags
-    causal = jnp.where(col_num <= row_num, keep, drop)
-    bias[0:ROWS, 3 * ROWS:] = causal
-    bias[ROWS:2 * ROWS, 3 * ROWS:] = causal
+        shown = jnp.full((1, ROWS), seen * inside, jnp.int32)
+        earlier[:, place_num * ROWS:(place_num + 1) * ROWS] = jnp.where(shown == 1, keep, drop)
+    causal = jnp.where(col_num <= row_num, F32(0), F32(-1e30))
+    bias[0:ROWS] = causal
+    bias[ROWS:2 * ROWS] = causal
 
     for copy in local_params:
         copy.wait()
@@ -411,6 +418,8 @@
                     def _():
                         copy_ahead.wait_send()
 
+    ones = jnp.ones((4 * ROWS, CHUNK), BF)
+
     def tick(t, carry):
         for step in range(HALO_PARTS):
             part = (x - zrow + step + 4) % 4
@@ -465,15 +474,18 @@
             def _():
                 extra_copy(t, part).wait_recv()
         norm(halo.at[t, 2], 2)
+        norm(halo.at[t, half], 1)
+        middle_rows = pl.ds(ROWS, 2 * ROWS)
+        project(0, middle_rows, keys)
+        project(1, middle_rows, values)
         for part in range(HALO_PARTS):
             @pl.when(seq > 0)
             def _():
                 forward_wait(t, part).wait_recv()
-        norm(halo.at[t, 0], 0)
-        norm(halo.at[t, 1], 1)
-        near_rows = pl.ds(0, 3 * ROWS)
-        project(0, near_rows, keys)
-        project(1, near_rows, values)
+        norm(halo.at[t, 1 - half], 0)
+        first_rows = pl.ds(0, ROWS)
+        project(0, first_rows, keys)
+        project(1, first_rows, values)
 
         def two_heads(k, carry):
             cols = pl.ds(pl.multiple_of(k * CHUNK, CHUNK), CHUNK)
@@ -481,15 +493,19 @@
             stacked = jnp.concatenate([both * pick_first, both * pick_second], axis=0)
             scores = lax.dot_general(
                 stacked, keys[:, cols], (((1,), (1,)), ((), ())), preferred_element_type=F32
-            ) + bias[...]
+            )
+            scores = jnp.concatenate(
+                [scores[:, :3 * ROWS] + earlier[...], scores[:, 3 * ROWS:] + bias[...]], axis=1
+            )
             top = jnp.max(scores, axis=-1, keepdims=True)
-            expo = jnp.exp(scores - top)
-            total = jnp.sum(expo, axis=-1, keepdims=True)
-            summed = jnp.dot(expo.astype(BF), values[:, cols], preferred_element_type=F32) / total
+            expo = jnp.exp(scores - top).astype(BF)
+            with_ones = jnp.concatenate([values[:, cols], ones], axis=1)
+            product = jnp.dot(expo, with_ones, preferred_element_type=F32)
+            summed = product[:, :CHUNK] / product[:, CHUNK:]
             attended[:, cols] = jnp.where(lane < 64, summed[:ROWS], summed[ROWS:]).astype(BF)
             return carry
 
-        lax.fori_loop(0, CHUNKS, two_heads, 0, unroll=4)
+        lax.fori_loop(0, CHUNKS, two_heads, 0, unroll=8)
         await_weight(t, 3)
 
         @pl.when(t > 0)
@@ -715,7 +731,8 @@
             pltpu.VMEM(block, BF),
             pltpu.VMEM((MIXES, 2, ROWS, ROWS), BF),
             pltpu.VMEM((MIXES, 4, CHUNK), F32),
-            pltpu.VMEM((2 * ROWS, 4 * ROWS), F32),
+            pltpu.VMEM((1, 3 * ROWS), F32),
+            pltpu.VMEM((2 * ROWS, ROWS), F32),
             pltpu.VMEM((TICKS - 1, 64, ROWS), BF),
             pltpu.VMEM((TICKS - 1, 64, ROWS), BF),
             pltpu.VMEM((TICKS - 1, ROWS, CHUNK), BF),

time: 144 us -> 139 us (0.965)
  Pallas kernels: 142 us -> 136 us
    pallas_call x1, Pallas kernels: 142 us -> 136 us  [local(): pl.pallas_call(kernel, out_shape=jax.ShapeDtypeStruct((1, 1, ROWS, WIDE),...]
where the time goes in v5:
time: 139 us; the launch traced here: 137 us
  Pallas kernels  136 us (98%)
  local copies, waits for them, and re-layouts  1.67 us (1%)
    pallas_call x1, Pallas kernels, local(): pl.pallas_call(kernel, out_shape=jax.ShapeDtypeStruct((1, 1, ROWS, WIDE),...  136 us

profile of v5, /device:TPU:481, one launch (start us, length us, event | category | flops | bytes accessed | tf_op | source)
XLA Modules:
  0.0 137.2 jit_solution(17046651710872158941)
XLA Ops:
  0.0 135.6 %shard_map.109 = bf16[1,1,128,1024]{3,2,1,0:T(8,128)(2,1)} custom-call(bf16[1,1,128,1024]{3,2,1,0:T(8,128)(2,1)} %start_ref.1, bf16[2,1,2,64,128]{4,3,2,1,0:T(8,128)(2,1)} %bitcast.3, f32[1,512]{1,0:T(1,128)} %gain_ref.1, bf16[1,512,1024]{2,1,0:T(8,128)(2,1)} %wq_ref.1, bf16[1,512,1024]{2,1,0:T(8,128)(2,1)} %wk_ref.1, bf16[1,512,1024]{2,1,0:T(8,128)(2,1)} %wv_ref.1, ...), custom_call_target="tpu_custom_call" | custom-call | tf_op jit(solution)/shard_map/pallas_call | solution.py:710
  135.6 1.7 %copy.13 = bf16[1,1,128,1024]{3,2,1,0:T(8,128)(2,1)} copy(bf16[1,1,128,1024]{3,2,1,0:T(8,128)(2,1)} %shard_map.109) | data formatting | bytes 524288

commit v6 on v5

--- a/solution.py
+++ b/solution.py
@@ -117,7 +117,7 @@
     feeds = jnp.logical_and(section != 7, section != FAR - 1)
     before = jnp.maximum(seq - 1, 0)
 
-    @pl.when(jnp.logical_and(fed, seq > 0))
+    @pl.when(jnp.logical_and(jnp.logical_and(fed, half == 1), seq > 0))
     def _():
         for f in range(CHUNKS):
             row = (before % 4 - f // 2 + 4) % 4
@@ -180,8 +180,8 @@
         + jnp.where(seq < 31, one, zero) + jnp.where(gives_extra, one, zero)
         + jnp.where(section > 0, one, zero)
         + jnp.where(section == FAR, 5 * one, zero)
-        + jnp.where(feeds, 8 * one, zero)
-        - jnp.where(jnp.logical_and(feeds, at_end), 2 * one, zero)
+        + jnp.where(feeds, 4 * one, zero)
+        - jnp.where(jnp.logical_and(feeds, at_end), one, zero)
     )
     pl.semaphore_wait(barrier, expected)
 
@@ -205,7 +205,7 @@
         )
 
     def by_neighbor(t):
-        return jnp.logical_or(t == 0, jnp.logical_not(fed))
+        return jnp.logical_or(t == 0, jnp.logical_not(jnp.logical_and(fed, half == 1)))
 
     def forward_copy(t, part):
         span = pl.ds(PER_PART * part, PER_PART)
@@ -380,12 +380,12 @@
     pick_first = first_head.astype(BF)
     pick_second = (1 - first_head).astype(BF)
 
-    def ahead_copy(t, k, m):
+    def ahead_copy(t, k):
         target = (zrow + k) % 4
-        c = (half + m) % 2
+        c = 1
         pair = 4 * (zbase + target) + held
         return pair, remote(
-            col_out.at[2 * target + c], halo.at[t + 1, c, mine], ahead_send.at[2 * k + m],
+            col_out.at[2 * target + c], halo.at[t + 1, c, mine], ahead_send.at[k],
             near_recv.at[t + 1, mine], 2 * section + 2 + c, jnp.minimum(pair + 1, 31),
         )
 
@@ -411,12 +411,11 @@
         @pl.when(jnp.logical_and(feeds, t < TICKS - 1))
         def _():
             for k in range(4):
-                for m in range(2):
-                    pair, copy_ahead = ahead_copy(t, k, m)
-
-                    @pl.when(pair < 31)
-                    def _():
-                        copy_ahead.wait_send()
+                pair, copy_ahead = ahead_copy(t, k)
+
+                @pl.when(pair < 31)
+                def _():
+                    copy_ahead.wait_send()
 
     ones = jnp.ones((4 * ROWS, CHUNK), BF)
 
@@ -622,12 +621,11 @@
         @pl.when(jnp.logical_and(feeds, t < TICKS - 1))
         def _():
             for k in range(4):
-                for m in range(2):
-                    pair, copy_ahead = ahead_copy(t, k, m)
-
-                    @pl.when(pair < 31)
-                    def _():
-                        copy_ahead.start()
+                pair, copy_ahead = ahead_copy(t, k)
+
+                @pl.when(pair < 31)
+                def _():
+                    copy_ahead.start()
 
         for part in range(HALO_PARTS):
             @pl.when(jnp.logical_and(seq < 31, by_neighbor(t)))
@@ -742,7 +740,7 @@
             dma((CHUNKS,)), dma, dma, dma((TICKS - 1, 2)), dma((TICKS - 1, 2)),
             dma((4,)), dma((4,)), dma((4,)), dma((3,)), dma((3,)), dma((3,)),
             dma, dma, dma((TICKS - 1,)),
-            dma((CHUNKS,)), dma((TICKS, CHUNKS)), dma((CHUNKS,)),
+            dma((CHUNKS,)), dma((TICKS, CHUNKS)), dma((4,)),
             dma((3, HALO_PARTS)), dma((TICKS, 3, HALO_PARTS)),
             dma((7,)), dma((TICKS, CHUNKS)),
             dma((3,)), dma((TICKS, 4)),

time: 139 us -> 137 us (0.986)
  no operation moved by 1% of the time
where the time goes in v6:
time: 137 us
  Pallas kernels  135 us (99%)
  local copies, waits for them, and re-layouts  1.67 us (1%)
    pallas_call x1, Pallas kernels, local(): pl.pallas_call(kernel, out_shape=jax.ShapeDtypeStruct((1, 1, ROWS, WIDE),...  135 us

profile of v6, /device:TPU:481, one launch (start us, length us, event | category | flops | bytes accessed | tf_op | source)
XLA Modules:
  0.0 136.6 jit_solution(8834316897710207333)
XLA Ops:
  0.0 134.9 %shard_map.109 = bf16[1,1,128,1024]{3,2,1,0:T(8,128)(2,1)} custom-call(bf16[1,1,128,1024]{3,2,1,0:T(8,128)(2,1)} %start_ref.1, bf16[2,1,2,64,128]{4,3,2,1,0:T(8,128)(2,1)} %bitcast.3, f32[1,512]{1,0:T(1,128)} %gain_ref.1, bf16[1,512,1024]{2,1,0:T(8,128)(2,1)} %wq_ref.1, bf16[1,512,1024]{2,1,0:T(8,128)(2,1)} %wk_ref.1, bf16[1,512,1024]{2,1,0:T(8,128)(2,1)} %wv_ref.1, ...), custom_call_target="tpu_custom_call" | custom-call | tf_op jit(solution)/shard_map/pallas_call | solution.py:708
  134.9 1.7 %copy.13 = bf16[1,1,128,1024]{3,2,1,0:T(8,128)(2,1)} copy(bf16[1,1,128,1024]{3,2,1,0:T(8,128)(2,1)} %shard_map.109) | data formatting | bytes 524288
